TPU v7x, 128 devices: a whole 4x4x4 slice. The times are simulated.
128 devices in a mesh: gx: 16 (over y, x), gy: 8 (over z, core).
Axes of the slice: x: 4, y: 4, z: 4, core: 2. Of those that a mesh axis runs over, the one named last changes fastest.
Arguments:
- atm_state: float32 [6, 786432], P(None, ('gx', 'gy')), may hold values from -6 to 6
- pair_block: int32 [32768], P(('gx', 'gy')), may hold values from 0 to 47
- pair_owner: int32 [32768, 1], P(('gx', 'gy')), may hold values from 0 to 127; in each aligned block of 256 rows (0 to 255, 256 to 511, ...) at most 4 rows name the same one
- pair_row: int32 [32768], P(('gx', 'gy')), may hold values from 0 to 63
- pair_tile: int32 [32768], P(('gx', 'gy')), may hold values from 0 to 127
- remap_weight: bfloat16 [16384, 128, 128], P(('gx', 'gy')), may hold values from 0.0014953613 to 0.029907227
- wet_mask: int32 [1024, 1024], P('gx', 'gy'), may hold values 0 or 1
- ocean_state: float32 [4, 16, 1024, 1024], P(None, None, 'gx', 'gy'), may hold values from -6 to 6
- vert_kappa: float32 [16, 1024, 1024], P(None, 'gx', 'gy'), may hold values from 0.05 to 3
- horiz_kappa: float32 [1024, 1024], P('gx', 'gy'), may hold values from 0.02 to 0.24
Outputs:
- ocean_next: float32 [4, 16, 1024, 1024], P(None, None, 'gx', 'gy')
- atm_surface: float32 [4, 786432], P(None, ('gx', 'gy'))
Inputs may be any that keep to these rules, and one draw needn't show every extreme that they name: `pair_owner`: the intersections of one device name one owner at most 4 times, and exactly 4 times for some owner.
All inputs are finite; a program needn't handle non-finite values. No bound on the sum of `wet_mask` on one device may be relied on, other than what follows from the above.
Results may differ from a plain program's by a relative error of at most 0.0039.
Values sent between devices are 32-bit elements; how exact they have to be, the bound alone decides.
A program may use at most 64 MiB of HBM per device.

v0:
```python
import jax
import jax.numpy as jnp
from jax import lax
from jax.sharding import PartitionSpec as P


def extended(shard, sides, width):
    for axis, dim in sides:
        count, length = (lax.axis_size(axis), shard.shape[dim])
        up = [(i, (i + 1) % count) for i in range(count - 1)]
        down = [(j, i) for i, j in up]
        last = lax.slice_in_dim(shard, length - width, length, axis=dim)
        leading = lax.slice_in_dim(shard, 0, width, axis=dim)
        before = lax.ppermute(last, axis, up)
        after = lax.ppermute(leading, axis, down)
        shard = jnp.concatenate([before, shard, after], axis=dim)
    return shard


def surface_flux(atm_state):
    wind_u = atm_state[0]
    wind_v = atm_state[1]
    speed = jnp.sqrt(wind_u * wind_u + wind_v * wind_v + 0.25)
    heat_flux = 0.5 * speed * (atm_state[2] - atm_state[5])
    water_flux = atm_state[4] - 0.3 * speed * atm_state[3]
    return jnp.stack([heat_flux, water_flux, 0.2 * speed * wind_u, 0.2 * speed * wind_v]).astype(
        jnp.bfloat16
    )


def column_mix(fields, vert_kappa):
    levels = vert_kappa.shape[0]
    face_coef = 0.5 * (vert_kappa[:-1] + vert_kappa[1:])
    zero_plane = jnp.zeros_like(vert_kappa[:1])
    above = jnp.concatenate([zero_plane, face_coef], 0)
    below = jnp.concatenate([face_coef, zero_plane], 0)
    diagonal = 1.0 + above + below
    upper_list = []
    rhs_list = []
    for level_index in range(levels):
        if level_index == 0:
            pivot_inv = 1.0 / diagonal[0]
            rhs_now = fields[:, 0] * pivot_inv
        else:
            pivot_inv = 1.0 / (diagonal[level_index] + above[level_index] * upper_list[-1])
            rhs_now = (fields[:, level_index] + above[level_index] * rhs_list[-1]) * pivot_inv
        upper_list.append(-below[level_index] * pivot_inv)
        rhs_list.append(rhs_now)
    solved = [rhs_list[-1]]
    for level_index in range(levels - 2, -1, -1):
        solved.append(rhs_list[level_index] - upper_list[level_index] * solved[-1])
    return jnp.stack(solved[::-1], 1)


def shifted(array, step_x, step_y):
    size_x = array.shape[-2]
    size_y = array.shape[-1]
    return array[..., 1 + step_x : size_x - 1 + step_x, 1 + step_y : size_y - 1 + step_y]


def diffuse(padded, coefficients):
    kappa_pad = coefficients[0]
    wet_pad = coefficients[1]
    centre = shifted(padded, 0, 0)
    kappa_mid = shifted(kappa_pad, 0, 0)
    wet_mid = shifted(wet_pad, 0, 0)
    result = centre
    for step_x, step_y in ((1, 0), (-1, 0), (0, 1), (0, -1)):
        face_coef = (
            0.25
            * (kappa_mid + shifted(kappa_pad, step_x, step_y))
            * wet_mid
            * shifted(wet_pad, step_x, step_y)
        )
        result = result + face_coef * (shifted(padded, step_x, step_y) - centre)
    return result


def local(
    atm_state,
    pair_block,
    pair_owner,
    pair_row,
    pair_tile,
    remap_weight,
    wet_mask,
    ocean_state,
    vert_kappa,
    horiz_kappa,
):
    highest = lax.Precision.HIGHEST
    grid_x = lax.axis_size("gx")
    grid_y = lax.axis_size("gy")
    devices = grid_x * grid_y
    npairs = pair_block.shape[0]
    capacity = max(2, 2 * npairs // devices)
    slot_count = devices * capacity
    tile_rows = ocean_state.shape[2]
    patch_width = ocean_state.shape[3]
    block_cols = remap_weight.shape[1]
    fluxes = surface_flux(atm_state)
    nblocks = fluxes.shape[1] // block_cols
    blocks = fluxes.reshape(4, nblocks, block_cols).transpose(1, 0, 2)
    tile_weights = remap_weight[pair_tile]
    contrib = jnp.einsum(
        "pca,pab->pcb", blocks[pair_block], tile_weights, preferred_element_type=jnp.float32
    )
    owner_ids = pair_owner[:, 0]
    owner_hits = (owner_ids[:, None] == jnp.arange(devices, dtype=jnp.int32)[None, :]).astype(
        jnp.int32
    )
    slot_rank = jnp.sum(owner_hits * (jnp.cumsum(owner_hits, 0) - 1), 1)
    send_slot = owner_ids * capacity + slot_rank
    outgoing = jnp.zeros((slot_count, 4, patch_width), jnp.float32).at[send_slot].set(contrib)
    out_rows = jnp.zeros((slot_count,), jnp.int32).at[send_slot].set(pair_row)
    arrived, in_rows = (
        lax.all_to_all(outgoing, ("gx", "gy"), split_axis=0, concat_axis=0, tiled=True),
        lax.all_to_all(out_rows, ("gx", "gy"), split_axis=0, concat_axis=0, tiled=True),
    )
    placing = (jnp.arange(tile_rows, dtype=jnp.int32)[:, None] == in_rows[None, :]).astype(
        jnp.float32
    )
    forcing = jnp.dot(
        placing,
        arrived.reshape(slot_count, 4 * patch_width),
        precision=highest,
        preferred_element_type=jnp.float32,
    )
    forcing = forcing.reshape(tile_rows, 4, patch_width).transpose(1, 0, 2)
    wet_frac = wet_mask.astype(jnp.float32)
    forced = ocean_state.at[:, 0].add(forcing * wet_frac[None])
    coef_pad = extended(jnp.stack([horiz_kappa, wet_frac]), (("gx", 1), ("gy", 2)), 2)
    coef_near = coef_pad[:, 1:-1, 1:-1]
    mixed = column_mix(forced, vert_kappa)
    tracers = mixed[:2]
    for pass_index in range(2):
        padded = extended(tracers, (("gx", 2), ("gy", 3)), 1)
        tracers = diffuse(padded, coef_near)
    ocean_next = jnp.concatenate([tracers, mixed[2:]], 0)
    surface = jnp.concatenate([ocean_next[:, 0] * wet_frac[None], wet_frac[None]], 0)
    sendback = surface.transpose(1, 0, 2)[in_rows]
    returned = lax.all_to_all(sendback, ("gx", "gy"), split_axis=0, concat_axis=0, tiled=True)
    picks = returned[send_slot]
    picks_high = picks.astype(jnp.bfloat16)
    picks_low = (picks - picks_high.astype(jnp.float32)).astype(jnp.bfloat16)
    back = jnp.einsum("pab,pcb->pca", tile_weights, picks_high, preferred_element_type=jnp.float32)
    back = back + jnp.einsum(
        "pab,pcb->pca", tile_weights, picks_low, preferred_element_type=jnp.float32
    )
    member = (jnp.arange(nblocks, dtype=jnp.int32)[:, None] == pair_block[None, :]).astype(
        jnp.float32
    )
    sums = jnp.dot(
        member,
        back.reshape(npairs, 5 * block_cols),
        precision=highest,
        preferred_element_type=jnp.float32,
    )
    sums = sums.reshape(nblocks, 5, block_cols)
    values = sums[:, :4] / jnp.maximum(sums[:, 4:5], 0.1)
    atm_surface = values.transpose(1, 0, 2).reshape(4, nblocks * block_cols)
    return (ocean_next, atm_surface)


def solution(mesh):
    placed = (
        P(None, ("gx", "gy")),
        P(("gx", "gy")),
        P(("gx", "gy"), None),
        P(("gx", "gy")),
        P(("gx", "gy")),
        P(("gx", "gy"), None, None),
        P("gx", "gy"),
        P(None, None, "gx", "gy"),
        P(None, "gx", "gy"),
        P("gx", "gy"),
    )
    return jax.shard_map(
        local,
        mesh=mesh,
        in_specs=placed,
        out_specs=(P(None, None, "gx", "gy"), P(None, ("gx", "gy"))),
        check_vma=False,
    )
```

profile of v0, /device:TPU:1, one launch (start us, length us, event | category | flops | bytes accessed | tf_op | source)
XLA Modules:
  0.0 219.5 jit_solution(2154435752038831250)
XLA Ops:
  0.6 0.8 copy.56
  1.8 0.9 fusion.50
  2.6 0.7 compare_select_fusion.1
  3.3 1.6 scatter_custom_fusion
  4.9 0.7 all_to_all.14
  5.6 11.5 %all-to-all-start = ((s32[128,4,1]{1,2,0:T(1,128)}), s32[128,4,1]{1,2,0:T(1,128)S(1)}, u32[]{:S(2)}, u32[]{:S(2)}) async-start(s32[128,4,1]{1,2,0:T(1,128)} %bitcast.7), calls=%async_computation | async-start | bytes 131072 | tf_op jit(solution)/shard_map/all_to_all | solution.py:118
  17.1 0.8 convert_bitcast_fusion.4
  17.9 0.7 pad_maximum_fusion.22
  18.6 3.3 %collective-permute-start = (f32[2,2,128]{2,1,0:T(2,128)S(1)}, f32[2,2,128]{2,1,0:T(2,128)S(1)}, u32[]{:S(2)}, u32[]{:S(2)}) collective-permute-start(f32[2,2,128]{2,1,0:T(2,128)S(1)} %get-tuple-element.104), channel_id=1, source_target_pairs={{0,8},{8,16},{16,24},{24,32},{32,40},{40,48},{48,56},{56,64},{64,7... | collective-permute-start | bytes 6152 | tf_op jit(solution)/shard_map/ppermute | solution.py:14
  21.9 1.4 collective-permute-start.1
  23.3 1.4 add_multiply_fusion
  24.8 0.6 fusion.92
  25.4 0.6 fusion.94
  26.0 0.6 fusion.96
  26.6 0.6 fusion.98
  27.3 0.6 fusion.100
  27.9 0.6 fusion.102
  28.5 0.6 fusion.104
  29.5 0.8 slice_bitcast_fusion.16
  30.4 1.0 gather_fusion
  32.1 10.9 %gather_fusion.1 = bf16[256,128,128]{2,1,0:T(8,128)(2,1)} fusion(bf16[128,128,128]{2,1,0:T(8,128)(2,1)} %param.17, s32[1024]{0:T(1024)S(1)} %get-tuple-element.109), kind=kCustom, calls=%fused_computation.1 | custom fusion | bytes 16778240 | tf_op jit(solution)/shard_map/gather | solution.py:104
  43.0 5.6 %fusion.138 = f32[256,4,128]{2,1,0:T(4,128)S(1)} fusion(bf16[256,4,128]{2,1,0:T(4,128)(2,1)S(1)} %gather_fusion, bf16[256,128,128]{2,1,0:T(8,128)(2,1)} %gather_fusion.1), kind=kOutput, calls=%fused_computation.271 | convolution fusion | flops 33554432 | bytes 9175040 | tf_op jit(solution)/shard_map/pca,pab->pcb/dot_general | solution.py:105
  48.7 1.1 broadcast_in_dim.8
  49.8 25.9 %scatter_fusion = f32[512,4,128]{2,1,0:T(4,128)} fusion(f32[512,4,128]{2,1,0:T(4,128)} %broadcast_in_dim.8, s32[256]{0:T(256)S(1)} %bitcast.297, f32[256,4,128]{2,1,0:T(4,128)S(1)} %fusion.138), kind=kCustom, calls=%fused_computation.5 | custom fusion | bytes 1573888 | tf_op jit(solution)/shard_map/scatter | solution.py:114
  75.7 11.0 %all-to-all-start.1 = ((f32[512,4,128]{2,1,0:T(4,128)}), f32[512,4,128]{2,1,0:T(4,128)S(1)}, u32[]{:S(2)}, u32[]{:S(2)}) async-start(f32[512,4,128]{2,1,0:T(4,128)} %scatter_fusion), calls=%async_computation.1 | async-start | bytes 2097152 | tf_op jit(solution)/shard_map/all_to_all | solution.py:117
  86.7 0.6 fusion.105
  87.4 3.7 %collective-permute-start.2 = (f32[2,68,2]{2,1,0:T(8,128)S(1)}, f32[2,68,2]{2,1,0:T(8,128)S(1)}, u32[]{:S(2)}, u32[]{:S(2)}) collective-permute-start(f32[2,68,2]{2,1,0:T(8,128)S(1)} %get-tuple-element.102), channel_id=1, source_target_pairs={{0,1},{1,2},{2,3},{3,4},{4,5},{5,6},{6,7},{8,9},{9,10},{10,11},{11... | collective-permute-start | bytes 3272 | tf_op jit(solution)/shard_map/ppermute | solution.py:14
  91.1 1.9 collective-permute-start.3
  93.0 0.7 fusion.76
  94.3 0.8 reduce.7
  95.2 1.3 collective-permute-done.2
  96.5 2.6 %collective-permute-done.3 = f32[2,68,2]{2,1,0:T(8,128)S(1)} collective-permute-done((f32[2,68,2]{2,1,0:T(8,128)S(1)}, f32[2,68,2]{2,1,0:T(8,128)S(1)}, u32[]{:S(2)}, u32[]{:S(2)}) %collective-permute-start.3) | collective-permute-done | bytes 1120 | tf_op jit(solution)/shard_map/ppermute | solution.py:15
  99.3 6.5 %all-to-all-done.1 = f32[512,4,128]{2,1,0:T(4,128)S(1)} async-done(((f32[512,4,128]{2,1,0:T(4,128)}), f32[512,4,128]{2,1,0:T(4,128)S(1)}, u32[]{:S(2)}, u32[]{:S(2)}) %all-to-all-start.1) | async-done | bytes 1048608 | tf_op jit(solution)/shard_map/all_to_all | solution.py:117
  106.3 2.9 %subtract_dynamic-update-slice_fusion = (f32[4,16,64,128]{3,2,0,1:T(8,128)S(1)}, f32[4,1,64,128]{3,2,0,1:T(8,128)S(1)}, f32[4,1,64,128]{3,2,0,1:T(8,128)S(1)}, f...) fusion(f32[64,128]{1,0:T(8,128)S(1)} %copy-done.18, ...), kind=kOutput, calls=%fused_computation.103 | convolution fusion | flops 203915264 | bytes 6653952 | tf_op jit(solution)/shard_map/dot_general | solution.py:123
  110.2 1.0 fusion.54
  111.3 1.3 collective-permute-start.4
  112.6 4.2 %collective-permute-start.5 = (f32[2,16,1,128]{3,2,0,1:T(1,128)S(1)}, f32[2,16,1,128]{3,2,0,1:T(1,128)S(1)}, u32[]{:S(2)}, u32[]{:S(2)}) collective-permute-start(f32[2,16,1,128]{3,2,0,1:T(1,128)S(1)} %get-tuple-element.59), channel_id=1, source_target_pairs={{0,8},{8,16},{16,24},{24,32},{32,40},{40,48},{48,56},{56,64},{64,7... | collective-permute-start | bytes 49160 | tf_op jit(solution)/shard_map/ppermute | solution.py:14
  117.5 1.4 fusion.135
  118.9 1.7 copy.75
  120.6 4.2 %collective-permute-start.6 = (f32[2,16,66,1]{2,1,3,0:T(8,128)S(1)}, f32[2,16,66,1]{2,1,3,0:T(8,128)S(1)}, u32[]{:S(2)}, u32[]{:S(2)}) collective-permute-start(f32[2,16,66,1]{2,1,3,0:T(8,128)S(1)} %copy.75), channel_id=1, source_target_pairs={{1,0},{2,1},{3,2},{4,3},{5,4},{6,5},{7,6},{9,8},{10,9},{11,10},{12... | collective-permute-start | bytes 25352 | tf_op jit(solution)/shard_map/ppermute | solution.py:15
  124.9 1.0 copy.77
  125.9 1.9 collective-permute-start.7
  128.0 1.5 copy.76
  129.5 1.5 copy.78
  131.0 2.8 %fusion.17 = f32[2,16,64,128]{3,2,0,1:T(8,128)S(1)} fusion(f32[2,16,64,128]{3,2,0,1:T(8,128)S(1)} %get-tuple-element.61, f32[2,16,66,1]{3,2,0,1:T(8,128)} %copy.78, f32[2,16,1,128]{3,2,0,1:T(1,128)S(1)} %collective-permute-done.4, f32[2,16,1,128]{3,2,0,1:T(1,128)S(1)} %collective-permute-done.5, f32[2,16,66,1]{3,2,0,1:T(8,128)} %copy.76, ...), kind=kLoop, calls=%fused_computation.39 | loop fusion | flops 5242880 | bytes 2277888 | tf_op jit(solution)/shard_map/add | solution.py:75
  133.8 1.3 collective-permute-start.8
  135.1 4.5 %collective-permute-start.9 = (f32[2,16,1,128]{3,2,0,1:T(1,128)S(1)}, f32[2,16,1,128]{3,2,0,1:T(1,128)S(1)}, u32[]{:S(2)}, u32[]{:S(2)}) collective-permute-start(f32[2,16,1,128]{3,2,0,1:T(1,128)S(1)} %get-tuple-element.67), channel_id=1, source_target_pairs={{0,8},{8,16},{16,24},{24,32},{32,40},{40,48},{48,56},{56,64},{64,7... | collective-permute-start | bytes 49160 | tf_op jit(solution)/shard_map/ppermute | solution.py:14
  139.7 0.8 collective-permute-done.9
  140.6 1.8 fusion.134
  142.4 1.7 copy.79
  144.1 3.3 %collective-permute-start.10 = (f32[2,16,66,1]{2,1,3,0:T(8,128)S(1)}, f32[2,16,66,1]{2,1,3,0:T(8,128)S(1)}, u32[]{:S(2)}, u32[]{:S(2)}) collective-permute-start(f32[2,16,66,1]{2,1,3,0:T(8,128)S(1)} %copy.79), channel_id=1, source_target_pairs={{1,0},{2,1},{3,2},{4,3},{5,4},{6,5},{7,6},{9,8},{10,9},{11,10},{12... | collective-permute-start | bytes 25352 | tf_op jit(solution)/shard_map/ppermute | solution.py:15
  147.4 1.7 copy.81
  149.1 3.1 %collective-permute-start.11 = (f32[2,16,66,1]{2,1,3,0:T(8,128)S(1)}, f32[2,16,66,1]{2,1,3,0:T(8,128)S(1)}, u32[]{:S(2)}, u32[]{:S(2)}) collective-permute-start(f32[2,16,66,1]{2,1,3,0:T(8,128)S(1)} %copy.81), channel_id=1, source_target_pairs={{0,1},{1,2},{2,3},{3,4},{4,5},{5,6},{6,7},{8,9},{9,10},{10,11},{11... | collective-permute-start | bytes 25352 | tf_op jit(solution)/shard_map/ppermute | solution.py:14
  152.2 1.5 copy.80
  153.7 1.5 copy.82
  155.2 2.8 %fusion.5 = f32[2,16,64,128]{3,2,0,1:T(8,128)S(1)} fusion(f32[2,16,64,128]{3,2,0,1:T(8,128)S(1)} %fusion.17, f32[2,16,66,1]{3,2,0,1:T(8,128)} %copy.82, f32[2,16,1,128]{3,2,0,1:T(1,128)S(1)} %collective-permute-done.8, f32[2,16,1,128]{3,2,0,1:T(1,128)S(1)} %collective-permute-done.9, f32[2,16,66,1]{3,2,0,1:T(8,128)} %copy.80, ...), kind=kLoop, calls=%fused_computation.19 | loop fusion | flops 5242880 | bytes 2277888 | tf_op jit(solution)/shard_map/add | solution.py:75
  158.7 2.7 %gather_fusion.2 = f32[512,5,128]{2,1,0:T(8,128)} fusion(f32[64,5,128]{2,1,0:T(8,128)S(1)} %copy.83, s32[1024]{0:T(1024)S(1)} %copy-done.19), kind=kCustom, calls=%fused_computation.2 | custom fusion | bytes 2623488 | tf_op jit(solution)/shard_map/gather | solution.py:141
  161.4 10.8 %all-to-all-start.2 = ((f32[512,5,128]{2,1,0:T(8,128)}), f32[512,5,128]{2,1,0:T(8,128)}, u32[]{:S(2)}, u32[]{:S(2)}) async-start(f32[512,5,128]{2,1,0:T(8,128)} %gather_fusion.2), calls=%async_computation.2 | async-start | bytes 4194304 | tf_op jit(solution)/shard_map/all_to_all | solution.py:142
  172.4 1.5 copy.85
  173.9 28.3 %all-to-all-done.2 = f32[512,5,128]{2,1,0:T(8,128)} async-done(((f32[512,5,128]{2,1,0:T(8,128)}), f32[512,5,128]{2,1,0:T(8,128)}, u32[]{:S(2)}, u32[]{:S(2)}) %all-to-all-start.2) | async-done | bytes 1310752 | tf_op jit(solution)/shard_map/all_to_all | solution.py:142
  202.2 2.3 %gather_fusion.3 = f32[256,5,128]{2,1,0:T(8,128)S(1)} fusion(f32[512,5,128]{2,1,0:T(8,128)} %all-to-all-done.2, s32[1024]{0:T(1024)S(1)} %pad_clamp_fusion), kind=kCustom, calls=%fused_computation.3 | custom fusion | bytes 1311744 | tf_op jit(solution)/shard_map/gather | solution.py:143
  204.5 6.7 %fusion.31 = f32[256,5,128]{2,1,0:T(8,128)S(1)} fusion(bf16[256,128,128]{2,1,0:T(8,128)(2,1)} %gather_fusion.1, f32[256,5,128]{2,1,0:T(8,128)S(1)} %gather_fusion.3), kind=kOutput, calls=%fused_computation.63 | convolution fusion | flops 42106880 | bytes 9699328 | tf_op jit(solution)/shard_map/pab,pcb->pca/dot_general | solution.py:146
  211.2 6.7 %convolution_add_fusion = f32[256,5,128]{2,1,0:T(8,128)S(1)} fusion(f32[256,5,128]{2,1,0:T(8,128)S(1)} %fusion.31, bf16[256,128,128]{2,1,0:T(8,128)(2,1)} %gather_fusion.1, f32[256,5,128]{2,1,0:T(8,128)S(1)} %gather_fusion.3), kind=kOutput, calls=%fused_computation.9 | convolution fusion | flops 42762240 | bytes 10354688 | tf_op jit(solution)/shard_map/pab,pcb->pca/dot_general | solution.py:147
  218.8 0.7 copy.105
  (112 shorter events, 6.3 us)
Async XLA Ops:
  3.3 46.5 %copy-start.20 = (s32[256,1]{0,1:T(1,128)}, s32[256,1]{0,1:T(1,128)S(1)}, u32[]{:S(2)}) copy-start(s32[256,1]{0,1:T(1,128)S(1)} %compare_select_fusion.1) | copy-start | bytes 3076
  5.6 25.8 %all-to-all-start = ((s32[128,4,1]{1,2,0:T(1,128)}), s32[128,4,1]{1,2,0:T(1,128)S(1)}, u32[]{:S(2)}, u32[]{:S(2)}) async-start(s32[128,4,1]{1,2,0:T(1,128)} %bitcast.7), calls=%async_computation | async-start | bytes 131072 | tf_op jit(solution)/shard_map/all_to_all | solution.py:118
  18.6 68.7 %collective-permute-start = (f32[2,2,128]{2,1,0:T(2,128)S(1)}, f32[2,2,128]{2,1,0:T(2,128)S(1)}, u32[]{:S(2)}, u32[]{:S(2)}) collective-permute-start(f32[2,2,128]{2,1,0:T(2,128)S(1)} %get-tuple-element.104), channel_id=1, source_target_pairs={{0,8},{8,16},{16,24},{24,32},{32,40},{40,48},{48,56},{56,64},{64,7... | collective-permute-start | bytes 6152 | tf_op jit(solution)/shard_map/ppermute | solution.py:14
  21.9 7.3 %copy-start.17 = (f32[6,6144]{1,0:T(8,128)S(1)}, f32[6,6144]{1,0:T(8,128)}, u32[]{:S(2)}) copy-start(f32[6,6144]{1,0:T(8,128)} %param.12) | copy-start | bytes 442372
  21.9 7.5 %copy-start.22 = (s32[256]{0:T(256)S(1)}, s32[256]{0:T(256)}, u32[]{:S(2)}) copy-start(s32[256]{0:T(256)} %param.13) | copy-start | bytes 3076
  21.9 7.6 %copy-start.24 = (s32[256]{0:T(256)S(1)}, s32[256]{0:T(256)}, u32[]{:S(2)}) copy-start(s32[256]{0:T(256)} %param.16) | copy-start | bytes 3076
  21.9 65.4 %collective-permute-start.1 = (f32[2,2,128]{2,1,0:T(2,128)S(1)}, f32[2,2,128]{2,1,0:T(2,128)S(1)}, u32[]{:S(2)}, u32[]{:S(2)}) collective-permute-start(f32[2,2,128]{2,1,0:T(2,128)S(1)} %get-tuple-element.105), channel_id=1, source_target_pairs={{8,0},{16,8},{24,16},{32,24},{40,32},{48,40},{56,48},{64,56},{72,6... | collective-permute-start | bytes 6152 | tf_op jit(solution)/shard_map/ppermute | solution.py:15
  25.4 17.6 %copy-start.6 = (f32[1,64,128]{2,1,0:T(8,128)}, f32[1,64,128]{2,1,0:T(8,128)S(1)}, u32[]{:S(2)}) copy-start(f32[1,64,128]{2,1,0:T(8,128)S(1)} %get-tuple-element.36) | copy-start | bytes 98308
  27.9 15.1 %copy-start = (f32[1,64,128]{2,1,0:T(8,128)}, f32[1,64,128]{2,1,0:T(8,128)S(1)}, u32[]{:S(2)}) copy-start(f32[1,64,128]{2,1,0:T(8,128)S(1)} %get-tuple-element.47) | copy-start | bytes 98308
  27.9 65.1 %copy-start.1 = (f32[1,64,128]{2,1,0:T(8,128)}, f32[1,64,128]{2,1,0:T(8,128)S(1)}, u32[]{:S(2)}) copy-start(f32[1,64,128]{2,1,0:T(8,128)S(1)} %get-tuple-element.48) | copy-start | bytes 98308
  28.5 14.5 %copy-start.3 = (f32[1,64,128]{2,1,0:T(8,128)}, f32[1,64,128]{2,1,0:T(8,128)S(1)}, u32[]{:S(2)}) copy-start(f32[1,64,128]{2,1,0:T(8,128)S(1)} %get-tuple-element.50) | copy-start | bytes 98308
  28.5 14.5 %copy-start.4 = (f32[1,64,128]{2,1,0:T(8,128)}, f32[1,64,128]{2,1,0:T(8,128)S(1)}, u32[]{:S(2)}) copy-start(f32[1,64,128]{2,1,0:T(8,128)S(1)} %get-tuple-element.51) | copy-start | bytes 98308
  29.2 13.8 %copy-start.5 = (f32[1,64,128]{2,1,0:T(8,128)}, f32[1,64,128]{2,1,0:T(8,128)S(1)}, u32[]{:S(2)}) copy-start(f32[1,64,128]{2,1,0:T(8,128)S(1)} %get-tuple-element.54) | copy-start | bytes 98308
  29.2 57.5 %copy-start.7 = (f32[1,64,128]{2,1,0:T(8,128)}, f32[1,64,128]{2,1,0:T(8,128)S(1)}, u32[]{:S(2)}) copy-start(f32[1,64,128]{2,1,0:T(8,128)S(1)} %get-tuple-element.53) | copy-start | bytes 98308
  49.8 37.6 %copy-start.16 = (f32[64,128]{1,0:T(8,128)S(1)}, f32[64,128]{1,0:T(8,128)}, u32[]{:S(2)}) copy-start(f32[64,128]{1,0:T(8,128)} %param.21) | copy-start | bytes 98308
  75.7 30.2 %all-to-all-start.1 = ((f32[512,4,128]{2,1,0:T(4,128)}), f32[512,4,128]{2,1,0:T(4,128)S(1)}, u32[]{:S(2)}, u32[]{:S(2)}) async-start(f32[512,4,128]{2,1,0:T(4,128)} %scatter_fusion), calls=%async_computation.1 | async-start | bytes 2097152 | tf_op jit(solution)/shard_map/all_to_all | solution.py:117
  87.4 9.1 %collective-permute-start.2 = (f32[2,68,2]{2,1,0:T(8,128)S(1)}, f32[2,68,2]{2,1,0:T(8,128)S(1)}, u32[]{:S(2)}, u32[]{:S(2)}) collective-permute-start(f32[2,68,2]{2,1,0:T(8,128)S(1)} %get-tuple-element.102), channel_id=1, source_target_pairs={{0,1},{1,2},{2,3},{3,4},{4,5},{5,6},{6,7},{8,9},{9,10},{10,11},{11... | collective-permute-start | bytes 3272 | tf_op jit(solution)/shard_map/ppermute | solution.py:14
  91.1 8.0 %collective-permute-start.3 = (f32[2,68,2]{2,1,0:T(8,128)S(1)}, f32[2,68,2]{2,1,0:T(8,128)S(1)}, u32[]{:S(2)}, u32[]{:S(2)}) collective-permute-start(f32[2,68,2]{2,1,0:T(8,128)S(1)} %get-tuple-element.103), channel_id=1, source_target_pairs={{1,0},{2,1},{3,2},{4,3},{5,4},{6,5},{7,6},{9,8},{10,9},{11,10},{12... | collective-permute-start | bytes 3272 | tf_op jit(solution)/shard_map/ppermute | solution.py:15
  93.7 12.5 %copy-start.2 = (f32[1,64,128]{2,1,0:T(8,128)S(1)}, f32[1,64,128]{2,1,0:T(8,128)}, u32[]{:S(2)}) copy-start(f32[1,64,128]{2,1,0:T(8,128)} %copy-done.1) | copy-start | bytes 98308
  95.1 11.2 %copy-start.8 = (f32[1,64,128]{2,1,0:T(8,128)S(1)}, f32[1,64,128]{2,1,0:T(8,128)}, u32[]{:S(2)}) copy-start(f32[1,64,128]{2,1,0:T(8,128)} %copy-done.7) | copy-start | bytes 98308
  95.1 11.2 %copy-start.18 = (f32[64,128]{1,0:T(8,128)S(1)}, f32[64,128]{1,0:T(8,128)}, u32[]{:S(2)}) copy-start(f32[64,128]{1,0:T(8,128)} %get-tuple-element.70) | copy-start | bytes 98308
  106.3 3.0 %copy-start.15 = (f32[64,128]{1,0:T(8,128)S(1)}, f32[64,128]{1,0:T(8,128)}, u32[]{:S(2)}) copy-start(f32[64,128]{1,0:T(8,128)} %get-tuple-element.35) | copy-start | bytes 98308
  106.3 3.1 %copy-start.14 = (f32[64,128]{1,0:T(8,128)S(1)}, f32[64,128]{1,0:T(8,128)}, u32[]{:S(2)}) copy-start(f32[64,128]{1,0:T(8,128)} %get-tuple-element.37) | copy-start | bytes 98308
  106.3 3.1 %copy-start.13 = (f32[64,128]{1,0:T(8,128)S(1)}, f32[64,128]{1,0:T(8,128)}, u32[]{:S(2)}) copy-start(f32[64,128]{1,0:T(8,128)} %get-tuple-element.40) | copy-start | bytes 98308
  109.2 0.8 copy-start.12
  109.2 0.8 copy-start.11
  109.3 0.8 copy-start.10
  109.3 0.9 copy-start.9
  111.3 5.7 %collective-permute-start.4 = (f32[2,16,1,128]{3,2,0,1:T(1,128)S(1)}, f32[2,16,1,128]{3,2,0,1:T(1,128)S(1)}, u32[]{:S(2)}, u32[]{:S(2)}) collective-permute-start(f32[2,16,1,128]{3,2,0,1:T(1,128)S(1)} %get-tuple-element.60), channel_id=1, source_target_pairs={{8,0},{16,8},{24,16},{32,24},{40,32},{48,40},{56,48},{64,56},{72,6... | collective-permute-start | bytes 49160 | tf_op jit(solution)/shard_map/ppermute | solution.py:15
  112.6 4.8 %collective-permute-start.5 = (f32[2,16,1,128]{3,2,0,1:T(1,128)S(1)}, f32[2,16,1,128]{3,2,0,1:T(1,128)S(1)}, u32[]{:S(2)}, u32[]{:S(2)}) collective-permute-start(f32[2,16,1,128]{3,2,0,1:T(1,128)S(1)} %get-tuple-element.59), channel_id=1, source_target_pairs={{0,8},{8,16},{16,24},{24,32},{32,40},{40,48},{48,56},{56,64},{64,7... | collective-permute-start | bytes 49160 | tf_op jit(solution)/shard_map/ppermute | solution.py:14
  120.6 7.4 %collective-permute-start.6 = (f32[2,16,66,1]{2,1,3,0:T(8,128)S(1)}, f32[2,16,66,1]{2,1,3,0:T(8,128)S(1)}, u32[]{:S(2)}, u32[]{:S(2)}) collective-permute-start(f32[2,16,66,1]{2,1,3,0:T(8,128)S(1)} %copy.75), channel_id=1, source_target_pairs={{1,0},{2,1},{3,2},{4,3},{5,4},{6,5},{7,6},{9,8},{10,9},{11,10},{12... | collective-permute-start | bytes 25352 | tf_op jit(solution)/shard_map/ppermute | solution.py:15
  125.9 3.6 %collective-permute-start.7 = (f32[2,16,66,1]{2,1,3,0:T(8,128)}, f32[2,16,66,1]{2,1,3,0:T(8,128)S(1)}, u32[]{:S(2)}, u32[]{:S(2)}) collective-permute-start(f32[2,16,66,1]{2,1,3,0:T(8,128)} %copy.77), channel_id=1, source_target_pairs={{0,1},{1,2},{2,3},{3,4},{4,5},{5,6},{6,7},{8,9},{9,10},{10,11},{11... | collective-permute-start | bytes 25352 | tf_op jit(solution)/shard_map/ppermute | solution.py:14
  133.8 5.9 %collective-permute-start.8 = (f32[2,16,1,128]{3,2,0,1:T(1,128)S(1)}, f32[2,16,1,128]{3,2,0,1:T(1,128)S(1)}, u32[]{:S(2)}, u32[]{:S(2)}) collective-permute-start(f32[2,16,1,128]{3,2,0,1:T(1,128)S(1)} %get-tuple-element.68), channel_id=1, source_target_pairs={{8,0},{16,8},{24,16},{32,24},{40,32},{48,40},{56,48},{64,56},{72,6... | collective-permute-start | bytes 49160 | tf_op jit(solution)/shard_map/ppermute | solution.py:15
  135.1 5.4 %collective-permute-start.9 = (f32[2,16,1,128]{3,2,0,1:T(1,128)S(1)}, f32[2,16,1,128]{3,2,0,1:T(1,128)S(1)}, u32[]{:S(2)}, u32[]{:S(2)}) collective-permute-start(f32[2,16,1,128]{3,2,0,1:T(1,128)S(1)} %get-tuple-element.67), channel_id=1, source_target_pairs={{0,8},{8,16},{16,24},{24,32},{32,40},{40,48},{48,56},{56,64},{64,7... | collective-permute-start | bytes 49160 | tf_op jit(solution)/shard_map/ppermute | solution.py:14
  144.1 8.1 %collective-permute-start.10 = (f32[2,16,66,1]{2,1,3,0:T(8,128)S(1)}, f32[2,16,66,1]{2,1,3,0:T(8,128)S(1)}, u32[]{:S(2)}, u32[]{:S(2)}) collective-permute-start(f32[2,16,66,1]{2,1,3,0:T(8,128)S(1)} %copy.79), channel_id=1, source_target_pairs={{1,0},{2,1},{3,2},{4,3},{5,4},{6,5},{7,6},{9,8},{10,9},{11,10},{12... | collective-permute-start | bytes 25352 | tf_op jit(solution)/shard_map/ppermute | solution.py:15
  149.1 4.7 %collective-permute-start.11 = (f32[2,16,66,1]{2,1,3,0:T(8,128)S(1)}, f32[2,16,66,1]{2,1,3,0:T(8,128)S(1)}, u32[]{:S(2)}, u32[]{:S(2)}) collective-permute-start(f32[2,16,66,1]{2,1,3,0:T(8,128)S(1)} %copy.81), channel_id=1, source_target_pairs={{0,1},{1,2},{2,3},{3,4},{4,5},{5,6},{6,7},{8,9},{9,10},{10,11},{11... | collective-permute-start | bytes 25352 | tf_op jit(solution)/shard_map/ppermute | solution.py:14
  158.0 0.7 copy-start.19
  161.4 10.9 %copy-start.21 = (s32[256,1]{0,1:T(1,128)S(1)}, s32[256,1]{0,1:T(1,128)}, u32[]{:S(2)}) copy-start(s32[256,1]{0,1:T(1,128)} %copy-done.20) | copy-start | bytes 3076
  161.4 40.7 %all-to-all-start.2 = ((f32[512,5,128]{2,1,0:T(8,128)}), f32[512,5,128]{2,1,0:T(8,128)}, u32[]{:S(2)}, u32[]{:S(2)}) async-start(f32[512,5,128]{2,1,0:T(8,128)} %gather_fusion.2), calls=%async_computation.2 | async-start | bytes 4194304 | tf_op jit(solution)/shard_map/all_to_all | solution.py:142
  211.2 7.1 %copy-start.23 = (s32[256]{0:T(256)S(1)}, s32[256]{0:T(256)}, u32[]{:S(2)}) copy-start(s32[256]{0:T(256)} %param.13) | copy-start | bytes 3076
where the time goes:
time: 221 us; the launch traced here: 219 us
  local copies, waits for them, and re-layouts  67.6 us (31%)
  starting transfers between devices  67.5 us (31%)
  waiting for transfers between devices  40 us (18%)
  matrix products  22.5 us (10%)
  other arithmetic  20.5 us (9%)
    all_to_all x1, waiting for transfers between devices, local(): lax.all_to_all(sendback, ('gx', 'gy'), split_axis=0, concat_axis=0, tiled...  28.3 us
    scatter x1, local copies, waits for them, and re-layouts, local(): jnp.zeros((slot_count, 4, patch_width), jnp.float32).at[send_slot]  25.9 us
    ppermute x6, starting transfers between devices, extended(): before = lax.ppermute(last, axis, up)  20.7 us
    ppermute x6, starting transfers between devices, extended(): after = lax.ppermute(leading, axis, down)  13.4 us
    all_to_all x1, starting transfers between devices, local(): lax.all_to_all(out_rows, ('gx', 'gy'), split_axis=0, concat_axis=0, tiled...  11.5 us
    all_to_all x1, starting transfers between devices, local(): lax.all_to_all(outgoing, ('gx', 'gy'), split_axis=0, concat_axis=0, tiled...  11 us
    gather x1, local copies, waits for them, and re-layouts, local(): tile_weights = remap_weight[pair_tile]  10.9 us
    all_to_all x1, starting transfers between devices, local(): lax.all_to_all(sendback, ('gx', 'gy'), split_axis=0, concat_axis=0, tiled...  10.8 us
  transfers between devices with their start and end apart: 15, of which 6 were waited for; matrix products, arithmetic and copies ran while one was open for 29% of the time, Pallas kernels for 0%

commit v1 on v0

--- a/solution.py
+++ b/solution.py
@@ -1,7 +1,69 @@
 import jax
 import jax.numpy as jnp
 from jax import lax
+from jax.experimental import pallas as pl
+from jax.experimental.pallas import tpu as pltpu
 from jax.sharding import PartitionSpec as P
+
+MESH = pl.DeviceIdType.MESH
+
+
+def exchange_kernel(x_ref, o_ref, buf, out_sem, in_sem, own_sem, ready):
+    gx, gy = lax.axis_index("gx"), lax.axis_index("gy")
+    barrier = pltpu.get_barrier_semaphore()
+    for r in range(1, 16):
+        pl.semaphore_signal(barrier, inc=1, device_id=((gx + r) % 16, gy), device_id_type=MESH)
+    for r in range(1, 8):
+        pl.semaphore_signal(barrier, inc=1, device_id=(gx, (gy + r) % 8), device_id_type=MESH)
+    pl.semaphore_wait(barrier, 22)
+    for r in range(1, 8):
+        pl.semaphore_signal(ready, inc=1, device_id=(gx, (gy + r) % 8), device_id_type=MESH)
+    pl.semaphore_wait(ready, 7)
+
+    def send(r, _):
+        dx, dy = (gx + r // 8) % 16, (gy + r % 8) % 8
+        pltpu.make_async_remote_copy(
+            src_ref=x_ref.at[dx * 8 + dy],
+            dst_ref=buf.at[r - 1],
+            send_sem=out_sem,
+            recv_sem=in_sem,
+            device_id=(dx, dy),
+            device_id_type=MESH,
+        ).start()
+        return 0
+
+    lax.fori_loop(1, 128, send, 0)
+    pltpu.make_async_copy(buf, buf, in_sem).wait()
+    pltpu.make_async_copy(buf, buf, out_sem).wait()
+    o_ref[gx * 8 + gy] = x_ref[gx * 8 + gy]
+
+    def put(r, _):
+        sx, sy = (gx + 16 - r // 8) % 16, (gy + 8 - r % 8) % 8
+        o_ref[sx * 8 + sy] = buf[r - 1]
+        return 0
+
+    lax.fori_loop(1, 128, put, 0)
+
+
+def exchange(x, number):
+    shape = x.shape
+    return pl.pallas_call(
+        exchange_kernel,
+        out_shape=jax.ShapeDtypeStruct(shape, x.dtype),
+        in_specs=[pl.BlockSpec(memory_space=pltpu.VMEM)],
+        out_specs=pl.BlockSpec(memory_space=pltpu.VMEM),
+        scratch_shapes=[
+            pltpu.VMEM((127,) + shape[1:], x.dtype),
+            pltpu.SemaphoreType.DMA,
+            pltpu.SemaphoreType.DMA,
+            pltpu.SemaphoreType.DMA,
+            pltpu.SemaphoreType.REGULAR,
+        ],
+        compiler_params=pltpu.CompilerParams(
+            collective_id=number, has_side_effects=True, vmem_limit_bytes=16 << 20
+        ),
+        name="exchange",
+    )(x)
 
 
 def extended(shard, sides, width):
@@ -114,7 +176,7 @@
     outgoing = jnp.zeros((slot_count, 4, patch_width), jnp.float32).at[send_slot].set(contrib)
     out_rows = jnp.zeros((slot_count,), jnp.int32).at[send_slot].set(pair_row)
     arrived, in_rows = (
-        lax.all_to_all(outgoing, ("gx", "gy"), split_axis=0, concat_axis=0, tiled=True),
+        exchange(outgoing.reshape(devices, capacity * 4, patch_width), 0),
         lax.all_to_all(out_rows, ("gx", "gy"), split_axis=0, concat_axis=0, tiled=True),
     )
     placing = (jnp.arange(tile_rows, dtype=jnp.int32)[:, None] == in_rows[None, :]).astype(
@@ -139,7 +201,7 @@
     ocean_next = jnp.concatenate([tracers, mixed[2:]], 0)
     surface = jnp.concatenate([ocean_next[:, 0] * wet_frac[None], wet_frac[None]], 0)
     sendback = surface.transpose(1, 0, 2)[in_rows]
-    returned = lax.all_to_all(sendback, ("gx", "gy"), split_axis=0, concat_axis=0, tiled=True)
+    returned = exchange(sendback.reshape(devices, capacity * 5, patch_width), 1).reshape(slot_count, 5, patch_width)
     picks = returned[send_slot]
     picks_high = picks.astype(jnp.bfloat16)
     picks_low = (picks - picks_high.astype(jnp.float32)).astype(jnp.bfloat16)

time: 221 us -> 211 us (0.955)
  Pallas kernels: 0 us -> 65.1 us
  waiting for transfers between devices: 40 us -> 0.85 us
  starting transfers between devices: 67.5 us -> 44.9 us
  local copies, waits for them, and re-layouts: 67.6 us -> 52.5 us
    pallas_call x0 -> x2, Pallas kernels: none -> 65.1 us  [exchange(): pl.pallas_call(exchange_kernel, out_shape=jax.ShapeDtypeStruct(shape, x.d...]
    all_to_all x2 -> x0, waiting for transfers between devices: 34.8 us -> none  [the longest x1 28.3 us: local(): lax.all_to_all(sendback, ('gx', 'gy'), split_axis=0, concat_axis=0, tiled...]
    all_to_all x2 -> x0, starting transfers between devices: 21.9 us -> none  [the longest x1 11 us: local(): lax.all_to_all(outgoing, ('gx', 'gy'), split_axis=0, concat_axis=0, tiled...]
    scatter x1, local copies, waits for them, and re-layouts: 25.9 us -> 6.97 us  [local(): jnp.zeros((slot_count, 4, patch_width), jnp.float32).at[send_slot]]
    ppermute x6, starting transfers between devices: 13.4 us -> 9.8 us  [extended(): after = lax.ppermute(leading, axis, down)]
    reshape x0 -> x2, local copies, waits for them, and re-layouts: none -> 3.2 us  [the longest x1 1.63 us: local(): sendback.reshape(devices, capacity * 5, patch_width)]
    ppermute x6, starting transfers between devices: 20.7 us -> 23.6 us  [extended(): before = lax.ppermute(last, axis, up)]
    ppermute x6, waiting for transfers between devices: 2.59 us -> 0.02 us  [extended(): after = lax.ppermute(leading, axis, down)]
  transfers between devices with their start and end apart: 15 -> 13, of which waited for: 6 -> 1; matrix products, arithmetic and copies ran while one was open for 29% -> 23% of each run, Pallas kernels for 0% -> 14%
where the time goes in v1:
time: 211 us; the launch traced here: 210 us
  Pallas kernels  65.1 us (31%)
  local copies, waits for them, and re-layouts  52.5 us (25%)
  starting transfers between devices  44.9 us (21%)
  matrix products  23.6 us (11%)
  other arithmetic  21.8 us (10%)
    pallas_call x2, Pallas kernels, exchange(): pl.pallas_call(exchange_kernel, out_shape=jax.ShapeDtypeStruct(shape, x.d...  65.1 us
    ppermute x6, starting transfers between devices, extended(): before = lax.ppermute(last, axis, up)  23.6 us
    all_to_all x1, starting transfers between devices, local(): lax.all_to_all(out_rows, ('gx', 'gy'), split_axis=0, concat_axis=0, tiled...  11.5 us
    gather x1, local copies, waits for them, and re-layouts, local(): tile_weights = remap_weight[pair_tile]  10.9 us
    ppermute x6, starting transfers between devices, extended(): after = lax.ppermute(leading, axis, down)  9.8 us
    scatter x1, local copies, waits for them, and re-layouts, local(): jnp.zeros((slot_count, 4, patch_width), jnp.float32).at[send_slot]  6.97 us
    dot_general x1, matrix products, local(): jnp.einsum('pab,pcb->pca', tile_weights, picks_low, preferred_element_typ...  6.75 us
    dot_general x1, matrix products, local(): jnp.einsum('pab,pcb->pca', tile_weights, picks_high, preferred_element_ty...  6.71 us
  transfers between devices with their start and end apart: 13, of which 1 were waited for; matrix products, arithmetic and copies ran while one was open for 23% of the time, Pallas kernels for 14%

profile of v1, /device:TPU:1, one launch (start us, length us, event | category | flops | bytes accessed | tf_op | source)
XLA Modules:
  0.0 210.1 jit_solution(1801837817789751018)
XLA Ops:
  0.6 0.8 copy.56
  1.8 0.9 fusion.49
  2.6 0.7 compare_select_fusion.1
  3.3 1.6 scatter_custom_fusion
  4.9 0.7 all_to_all.8
  5.6 11.5 %all-to-all-start = ((s32[128,4,1]{1,2,0:T(1,128)}), s32[128,4,1]{1,2,0:T(1,128)S(1)}, u32[]{:S(2)}, u32[]{:S(2)}) async-start(s32[128,4,1]{1,2,0:T(1,128)} %bitcast.7), calls=%async_computation | async-start | bytes 131072 | tf_op jit(solution)/shard_map/all_to_all | solution.py:180
  17.1 0.8 convert_bitcast_fusion.4
  17.9 1.3 pad_maximum_fusion.22
  19.2 3.3 %collective-permute-start = (f32[2,2,128]{2,1,0:T(2,128)}, f32[2,2,128]{2,1,0:T(2,128)S(1)}, u32[]{:S(2)}, u32[]{:S(2)}) collective-permute-start(f32[2,2,128]{2,1,0:T(2,128)} %get-tuple-element.104), channel_id=1, source_target_pairs={{0,8},{8,16},{16,24},{24,32},{32,40},{40,48},{48,56},{56,64},{64,7... | collective-permute-start | bytes 6152 | tf_op jit(solution)/shard_map/ppermute | solution.py:76
  22.5 1.4 collective-permute-start.1
  23.9 1.4 add_multiply_fusion
  25.3 0.6 fusion.91
  26.0 0.6 fusion.93
  26.6 0.6 fusion.95
  27.2 0.6 fusion.97
  27.9 0.6 fusion.99
  28.5 0.6 fusion.101
  29.7 0.6 fusion.104
  30.7 0.8 slice_bitcast_fusion.16
  31.6 1.0 gather_fusion
  32.6 10.9 %gather_fusion.1 = bf16[256,128,128]{2,1,0:T(8,128)(2,1)} fusion(bf16[128,128,128]{2,1,0:T(8,128)(2,1)} %param.17, s32[1024]{0:T(1024)S(1)} %get-tuple-element.110), kind=kCustom, calls=%fused_computation.1 | custom fusion | bytes 16778240 | tf_op jit(solution)/shard_map/gather | solution.py:166
  43.5 5.6 %fusion.137 = f32[256,4,128]{2,1,0:T(4,128)S(1)} fusion(bf16[256,4,128]{2,1,0:T(4,128)(2,1)S(1)} %gather_fusion, bf16[256,128,128]{2,1,0:T(8,128)(2,1)} %gather_fusion.1), kind=kOutput, calls=%fused_computation.270 | convolution fusion | flops 33554432 | bytes 9175040 | tf_op jit(solution)/shard_map/pca,pab->pcb/dot_general | solution.py:167
  49.1 0.7 fusion.75
  50.0 7.0 %scatter_fusion = f32[512,4,128]{2,1,0:T(4,128)S(1)} fusion(f32[512,4,128]{2,1,0:T(4,128)S(1)} %broadcast_in_dim.8, s32[256]{0:T(256)S(1)} %bitcast.295, f32[256,4,128]{2,1,0:T(4,128)S(1)} %fusion.137), kind=kCustom, calls=%fused_computation.5 | custom fusion | bytes 1573888 | tf_op jit(solution)/shard_map/scatter | solution.py:176
  57.0 29.9 %exchange.2 = f32[128,16,128]{2,1,0:T(8,128)S(1)} custom-call(f32[128,16,128]{2,1,0:T(8,128)S(1)} %bitcast.269), custom_call_target="tpu_custom_call" | custom-call | tf_op jit(solution)/shard_map/exchange/pallas_call | solution.py:50
  87.9 0.8 reduce.7
  88.8 2.9 %subtract_dynamic-update-slice_fusion = (f32[4,16,64,128]{3,2,0,1:T(8,128)S(1)}, f32[4,1,64,128]{3,2,0,1:T(8,128)S(1)}, f32[4,1,64,128]{3,2,0,1:T(8,128)S(1)}, f...) fusion(f32[64,128]{1,0:T(8,128)} %get-tuple-element.70, ...), kind=kOutput, calls=%fused_computation.102 | convolution fusion | flops 203915264 | bytes 6653952 | tf_op jit(solution)/shard_map/dot_general | solution.py:185
  92.8 1.0 fusion.53
  94.6 2.7 %collective-permute-start.2 = (f32[2,68,2]{2,1,0:T(8,128)S(1)}, f32[2,68,2]{2,1,0:T(8,128)S(1)}, u32[]{:S(2)}, u32[]{:S(2)}) collective-permute-start(f32[2,68,2]{2,1,0:T(8,128)S(1)} %get-tuple-element.102), channel_id=1, source_target_pairs={{0,1},{1,2},{2,3},{3,4},{4,5},{5,6},{6,7},{8,9},{9,10},{10,11},{11... | collective-permute-start | bytes 3272 | tf_op jit(solution)/shard_map/ppermute | solution.py:76
  97.3 1.9 collective-permute-start.3
  99.3 1.3 collective-permute-start.4
  100.6 4.2 %collective-permute-start.5 = (f32[2,16,1,128]{3,2,0,1:T(1,128)S(1)}, f32[2,16,1,128]{3,2,0,1:T(1,128)S(1)}, u32[]{:S(2)}, u32[]{:S(2)}) collective-permute-start(f32[2,16,1,128]{3,2,0,1:T(1,128)S(1)} %get-tuple-element.59), channel_id=1, source_target_pairs={{0,8},{8,16},{16,24},{24,32},{32,40},{40,48},{48,56},{56,64},{64,7... | collective-permute-start | bytes 49160 | tf_op jit(solution)/shard_map/ppermute | solution.py:76
  104.8 0.7 all_to_all.10
  105.9 1.4 fusion.134
  107.2 1.7 copy.75
  108.9 1.9 collective-permute-start.6
  110.9 1.0 copy.77
  111.9 4.5 %collective-permute-start.7 = (f32[2,16,66,1]{2,1,3,0:T(8,128)}, f32[2,16,66,1]{2,1,3,0:T(8,128)S(1)}, u32[]{:S(2)}, u32[]{:S(2)}) collective-permute-start(f32[2,16,66,1]{2,1,3,0:T(8,128)} %copy.77), channel_id=1, source_target_pairs={{0,1},{1,2},{2,3},{3,4},{4,5},{5,6},{6,7},{8,9},{9,10},{10,11},{11... | collective-permute-start | bytes 25352 | tf_op jit(solution)/shard_map/ppermute | solution.py:76
  116.5 1.5 copy.76
  118.1 1.5 copy.78
  119.6 2.8 %fusion.17 = f32[2,16,64,128]{3,2,0,1:T(8,128)S(1)} fusion(f32[2,16,64,128]{3,2,0,1:T(8,128)S(1)} %get-tuple-element.61, f32[2,16,66,1]{3,2,0,1:T(8,128)} %copy.78, f32[2,16,1,128]{3,2,0,1:T(1,128)S(1)} %collective-permute-done.4, f32[2,16,1,128]{3,2,0,1:T(1,128)S(1)} %collective-permute-done.5, f32[2,16,66,1]{3,2,0,1:T(8,128)} %copy.76, ...), kind=kLoop, calls=%fused_computation.39 | loop fusion | flops 5242880 | bytes 2277888 | tf_op jit(solution)/shard_map/add | solution.py:137
  122.4 1.3 collective-permute-start.8
  123.7 4.5 %collective-permute-start.9 = (f32[2,16,1,128]{3,2,0,1:T(1,128)S(1)}, f32[2,16,1,128]{3,2,0,1:T(1,128)S(1)}, u32[]{:S(2)}, u32[]{:S(2)}) collective-permute-start(f32[2,16,1,128]{3,2,0,1:T(1,128)S(1)} %get-tuple-element.67), channel_id=1, source_target_pairs={{0,8},{8,16},{16,24},{24,32},{32,40},{40,48},{48,56},{56,64},{64,7... | collective-permute-start | bytes 49160 | tf_op jit(solution)/shard_map/ppermute | solution.py:76
  128.3 0.8 collective-permute-done.9
  129.2 1.8 fusion.133
  131.0 1.7 copy.79
  132.7 1.9 collective-permute-start.10
  134.7 1.7 copy.81
  136.3 4.5 %collective-permute-start.11 = (f32[2,16,66,1]{2,1,3,0:T(8,128)S(1)}, f32[2,16,66,1]{2,1,3,0:T(8,128)S(1)}, u32[]{:S(2)}, u32[]{:S(2)}) collective-permute-start(f32[2,16,66,1]{2,1,3,0:T(8,128)S(1)} %copy.81), channel_id=1, source_target_pairs={{0,1},{1,2},{2,3},{3,4},{4,5},{5,6},{6,7},{8,9},{9,10},{10,11},{11... | collective-permute-start | bytes 25352 | tf_op jit(solution)/shard_map/ppermute | solution.py:76
  140.8 1.5 copy.80
  142.4 1.5 copy.82
  143.9 2.8 %fusion.5 = f32[2,16,64,128]{3,2,0,1:T(8,128)S(1)} fusion(f32[2,16,64,128]{3,2,0,1:T(8,128)S(1)} %fusion.17, f32[2,16,66,1]{3,2,0,1:T(8,128)} %copy.82, f32[2,16,1,128]{3,2,0,1:T(1,128)S(1)} %collective-permute-done.8, f32[2,16,1,128]{3,2,0,1:T(1,128)S(1)} %collective-permute-done.9, f32[2,16,66,1]{3,2,0,1:T(8,128)} %copy.80, ...), kind=kLoop, calls=%fused_computation.19 | loop fusion | flops 5242880 | bytes 2277888 | tf_op jit(solution)/shard_map/add | solution.py:137
  146.7 1.5 pad_maximum_fusion
  148.3 2.7 %gather_fusion.2 = f32[512,5,128]{2,1,0:T(8,128)} fusion(f32[64,5,128]{2,1,0:T(8,128)S(1)} %copy.83, s32[1024]{0:T(1024)S(1)} %get-tuple-element.109), kind=kCustom, calls=%fused_computation.2 | custom fusion | bytes 2623488 | tf_op jit(solution)/shard_map/gather | solution.py:203
  150.9 1.6 reshape.134.x_ref
  152.6 35.2 %exchange.3 = f32[128,20,128]{2,1,0:T(8,128)S(1)} custom-call(f32[128,20,128]{2,1,0:T(8,128)S(1)} %reshape.134.x_ref), custom_call_target="tpu_custom_call" | custom-call | tf_op jit(solution)/shard_map/exchange/pallas_call | solution.py:50
  187.8 1.6 reshape.135
  189.4 2.3 %gather_fusion.3 = f32[256,5,128]{2,1,0:T(8,128)S(1)} fusion(f32[512,5,128]{2,1,0:T(8,128)} %reshape.135, s32[1024]{0:T(1024)S(1)} %get-tuple-element.108), kind=kCustom, calls=%fused_computation.3 | custom fusion | bytes 1311744 | tf_op jit(solution)/shard_map/gather | solution.py:205
  191.7 6.7 %fusion.30 = f32[256,5,128]{2,1,0:T(8,128)S(1)} fusion(bf16[256,128,128]{2,1,0:T(8,128)(2,1)} %gather_fusion.1, f32[256,5,128]{2,1,0:T(8,128)S(1)} %gather_fusion.3), kind=kOutput, calls=%fused_computation.62 | convolution fusion | flops 42106880 | bytes 9699328 | tf_op jit(solution)/shard_map/pab,pcb->pca/dot_general | solution.py:208
  198.5 6.7 %convolution_add_fusion = f32[256,5,128]{2,1,0:T(8,128)S(1)} fusion(f32[256,5,128]{2,1,0:T(8,128)S(1)} %fusion.30, bf16[256,128,128]{2,1,0:T(8,128)(2,1)} %gather_fusion.1, f32[256,5,128]{2,1,0:T(8,128)S(1)} %gather_fusion.3), kind=kOutput, calls=%fused_computation.9 | convolution fusion | flops 42762240 | bytes 10354688 | tf_op jit(solution)/shard_map/pab,pcb->pca/dot_general | solution.py:209
  205.2 1.2 copy.84
  206.4 1.5 fusion.27
  208.0 0.7 copy.104
  208.6 1.5 copy.85
  (98 shorter events, 5.1 us)
Async XLA Ops:
  3.3 46.7 %copy-start.12 = (s32[256,1]{0,1:T(1,128)}, s32[256,1]{0,1:T(1,128)S(1)}, u32[]{:S(2)}) copy-start(s32[256,1]{0,1:T(1,128)S(1)} %compare_select_fusion.1) | copy-start | bytes 3076
  5.6 81.8 %all-to-all-start = ((s32[128,4,1]{1,2,0:T(1,128)}), s32[128,4,1]{1,2,0:T(1,128)S(1)}, u32[]{:S(2)}, u32[]{:S(2)}) async-start(s32[128,4,1]{1,2,0:T(1,128)} %bitcast.7), calls=%async_computation | async-start | bytes 131072 | tf_op jit(solution)/shard_map/all_to_all | solution.py:180
  19.2 74.9 %collective-permute-start = (f32[2,2,128]{2,1,0:T(2,128)}, f32[2,2,128]{2,1,0:T(2,128)S(1)}, u32[]{:S(2)}, u32[]{:S(2)}) collective-permute-start(f32[2,2,128]{2,1,0:T(2,128)} %get-tuple-element.104), channel_id=1, source_target_pairs={{0,8},{8,16},{16,24},{24,32},{32,40},{40,48},{48,56},{56,64},{64,7... | collective-permute-start | bytes 6152 | tf_op jit(solution)/shard_map/ppermute | solution.py:76
  22.4 7.9 %copy-start.11 = (f32[6,6144]{1,0:T(8,128)S(1)}, f32[6,6144]{1,0:T(8,128)}, u32[]{:S(2)}) copy-start(f32[6,6144]{1,0:T(8,128)} %param.12) | copy-start | bytes 442372
  22.5 71.6 %collective-permute-start.1 = (f32[2,2,128]{2,1,0:T(2,128)S(1)}, f32[2,2,128]{2,1,0:T(2,128)S(1)}, u32[]{:S(2)}, u32[]{:S(2)}) collective-permute-start(f32[2,2,128]{2,1,0:T(2,128)S(1)} %get-tuple-element.105), channel_id=1, source_target_pairs={{8,0},{16,8},{24,16},{32,24},{40,32},{48,40},{56,48},{64,56},{72,6... | collective-permute-start | bytes 6152 | tf_op jit(solution)/shard_map/ppermute | solution.py:77
  25.3 5.4 %copy-start.17 = (s32[256]{0:T(256)S(1)}, s32[256]{0:T(256)}, u32[]{:S(2)}) copy-start(s32[256]{0:T(256)} %param.16) | copy-start | bytes 3076
  25.3 5.4 %copy-start.15 = (s32[256]{0:T(256)S(1)}, s32[256]{0:T(256)}, u32[]{:S(2)}) copy-start(s32[256]{0:T(256)} %param.13) | copy-start | bytes 3076
  26.0 17.5 %copy-start.1 = (f32[1,64,128]{2,1,0:T(8,128)}, f32[1,64,128]{2,1,0:T(8,128)S(1)}, u32[]{:S(2)}) copy-start(f32[1,64,128]{2,1,0:T(8,128)S(1)} %get-tuple-element.36) | copy-start | bytes 98308
  29.7 13.7 %copy-start.2 = (f32[1,64,128]{2,1,0:T(8,128)}, f32[1,64,128]{2,1,0:T(8,128)S(1)}, u32[]{:S(2)}) copy-start(f32[1,64,128]{2,1,0:T(8,128)S(1)} %get-tuple-element.53) | copy-start | bytes 98308
  88.8 3.0 %copy-start.9 = (f32[64,128]{1,0:T(8,128)S(1)}, f32[64,128]{1,0:T(8,128)}, u32[]{:S(2)}) copy-start(f32[64,128]{1,0:T(8,128)} %get-tuple-element.35) | copy-start | bytes 98308
  88.8 3.1 %copy-start.8 = (f32[64,128]{1,0:T(8,128)S(1)}, f32[64,128]{1,0:T(8,128)}, u32[]{:S(2)}) copy-start(f32[64,128]{1,0:T(8,128)} %get-tuple-element.37) | copy-start | bytes 98308
  88.8 3.1 %copy-start.7 = (f32[64,128]{1,0:T(8,128)S(1)}, f32[64,128]{1,0:T(8,128)}, u32[]{:S(2)}) copy-start(f32[64,128]{1,0:T(8,128)} %get-tuple-element.40) | copy-start | bytes 98308
  91.8 0.8 copy-start.6
  91.8 0.8 copy-start.5
  91.8 0.8 copy-start.4
  91.8 0.9 copy-start.3
  93.8 0.8 copy-start.10
  94.6 10.8 %collective-permute-start.2 = (f32[2,68,2]{2,1,0:T(8,128)S(1)}, f32[2,68,2]{2,1,0:T(8,128)S(1)}, u32[]{:S(2)}, u32[]{:S(2)}) collective-permute-start(f32[2,68,2]{2,1,0:T(8,128)S(1)} %get-tuple-element.102), channel_id=1, source_target_pairs={{0,1},{1,2},{2,3},{3,4},{4,5},{5,6},{6,7},{8,9},{9,10},{10,11},{11... | collective-permute-start | bytes 3272 | tf_op jit(solution)/shard_map/ppermute | solution.py:76
  97.3 8.1 %collective-permute-start.3 = (f32[2,68,2]{2,1,0:T(8,128)S(1)}, f32[2,68,2]{2,1,0:T(8,128)S(1)}, u32[]{:S(2)}, u32[]{:S(2)}) collective-permute-start(f32[2,68,2]{2,1,0:T(8,128)S(1)} %get-tuple-element.103), channel_id=1, source_target_pairs={{1,0},{2,1},{3,2},{4,3},{5,4},{6,5},{7,6},{9,8},{10,9},{11,10},{12... | collective-permute-start | bytes 3272 | tf_op jit(solution)/shard_map/ppermute | solution.py:77
  99.3 6.4 %collective-permute-start.4 = (f32[2,16,1,128]{3,2,0,1:T(1,128)S(1)}, f32[2,16,1,128]{3,2,0,1:T(1,128)S(1)}, u32[]{:S(2)}, u32[]{:S(2)}) collective-permute-start(f32[2,16,1,128]{3,2,0,1:T(1,128)S(1)} %get-tuple-element.60), channel_id=1, source_target_pairs={{8,0},{16,8},{24,16},{32,24},{40,32},{48,40},{56,48},{64,56},{72,6... | collective-permute-start | bytes 49160 | tf_op jit(solution)/shard_map/ppermute | solution.py:77
  100.6 5.1 %collective-permute-start.5 = (f32[2,16,1,128]{3,2,0,1:T(1,128)S(1)}, f32[2,16,1,128]{3,2,0,1:T(1,128)S(1)}, u32[]{:S(2)}, u32[]{:S(2)}) collective-permute-start(f32[2,16,1,128]{3,2,0,1:T(1,128)S(1)} %get-tuple-element.59), channel_id=1, source_target_pairs={{0,8},{8,16},{16,24},{24,32},{32,40},{40,48},{48,56},{56,64},{64,7... | collective-permute-start | bytes 49160 | tf_op jit(solution)/shard_map/ppermute | solution.py:76
  108.9 7.6 %collective-permute-start.6 = (f32[2,16,66,1]{2,1,3,0:T(8,128)S(1)}, f32[2,16,66,1]{2,1,3,0:T(8,128)S(1)}, u32[]{:S(2)}, u32[]{:S(2)}) collective-permute-start(f32[2,16,66,1]{2,1,3,0:T(8,128)S(1)} %copy.75), channel_id=1, source_target_pairs={{1,0},{2,1},{3,2},{4,3},{5,4},{6,5},{7,6},{9,8},{10,9},{11,10},{12... | collective-permute-start | bytes 25352 | tf_op jit(solution)/shard_map/ppermute | solution.py:77
  111.9 6.1 %collective-permute-start.7 = (f32[2,16,66,1]{2,1,3,0:T(8,128)}, f32[2,16,66,1]{2,1,3,0:T(8,128)S(1)}, u32[]{:S(2)}, u32[]{:S(2)}) collective-permute-start(f32[2,16,66,1]{2,1,3,0:T(8,128)} %copy.77), channel_id=1, source_target_pairs={{0,1},{1,2},{2,3},{3,4},{4,5},{5,6},{6,7},{8,9},{9,10},{10,11},{11... | collective-permute-start | bytes 25352 | tf_op jit(solution)/shard_map/ppermute | solution.py:76
  119.6 8.7 %copy-start.14 = (s32[512,1]{0,1:T(1,128)S(1)}, s32[512,1]{0,1:T(1,128)}, u32[]{:S(2)}) copy-start(s32[512,1]{0,1:T(1,128)} %all_to_all.10) | copy-start | bytes 6148
  122.4 5.9 %collective-permute-start.8 = (f32[2,16,1,128]{3,2,0,1:T(1,128)S(1)}, f32[2,16,1,128]{3,2,0,1:T(1,128)S(1)}, u32[]{:S(2)}, u32[]{:S(2)}) collective-permute-start(f32[2,16,1,128]{3,2,0,1:T(1,128)S(1)} %get-tuple-element.68), channel_id=1, source_target_pairs={{8,0},{16,8},{24,16},{32,24},{40,32},{48,40},{56,48},{64,56},{72,6... | collective-permute-start | bytes 49160 | tf_op jit(solution)/shard_map/ppermute | solution.py:77
  123.7 5.4 %collective-permute-start.9 = (f32[2,16,1,128]{3,2,0,1:T(1,128)S(1)}, f32[2,16,1,128]{3,2,0,1:T(1,128)S(1)}, u32[]{:S(2)}, u32[]{:S(2)}) collective-permute-start(f32[2,16,1,128]{3,2,0,1:T(1,128)S(1)} %get-tuple-element.67), channel_id=1, source_target_pairs={{0,8},{8,16},{16,24},{24,32},{32,40},{40,48},{48,56},{56,64},{64,7... | collective-permute-start | bytes 49160 | tf_op jit(solution)/shard_map/ppermute | solution.py:76
  131.0 9.8 %copy-start.13 = (s32[256,1]{0,1:T(1,128)S(1)}, s32[256,1]{0,1:T(1,128)}, u32[]{:S(2)}) copy-start(s32[256,1]{0,1:T(1,128)} %copy-done.12) | copy-start | bytes 3076
  132.7 8.1 %collective-permute-start.10 = (f32[2,16,66,1]{2,1,3,0:T(8,128)S(1)}, f32[2,16,66,1]{2,1,3,0:T(8,128)S(1)}, u32[]{:S(2)}, u32[]{:S(2)}) collective-permute-start(f32[2,16,66,1]{2,1,3,0:T(8,128)S(1)} %copy.79), channel_id=1, source_target_pairs={{1,0},{2,1},{3,2},{4,3},{5,4},{6,5},{7,6},{9,8},{10,9},{11,10},{12... | collective-permute-start | bytes 25352 | tf_op jit(solution)/shard_map/ppermute | solution.py:77
  136.3 6.0 %collective-permute-start.11 = (f32[2,16,66,1]{2,1,3,0:T(8,128)S(1)}, f32[2,16,66,1]{2,1,3,0:T(8,128)S(1)}, u32[]{:S(2)}, u32[]{:S(2)}) collective-permute-start(f32[2,16,66,1]{2,1,3,0:T(8,128)S(1)} %copy.81), channel_id=1, source_target_pairs={{0,1},{1,2},{2,3},{3,4},{4,5},{5,6},{6,7},{8,9},{9,10},{10,11},{11... | collective-permute-start | bytes 25352 | tf_op jit(solution)/shard_map/ppermute | solution.py:76
  198.5 7.9 %copy-start.16 = (s32[256]{0:T(256)S(1)}, s32[256]{0:T(256)}, u32[]{:S(2)}) copy-start(s32[256]{0:T(256)} %param.13) | copy-start | bytes 3076
  205.2 3.4 %copy-start = (f32[4,16,64,128]{3,2,0,1:T(8,128)S(1)}, f32[4,16,64,128]{3,2,0,1:T(8,128)}, u32[]{:S(2)}) copy-start(f32[4,16,64,128]{3,2,0,1:T(8,128)} %pad_maximum_fusion) | copy-start | bytes 6291460

commit v2 on v0

v2 whole, which is shorter than its diff:
```python
import functools
import itertools
import random

import jax
import jax.numpy as jnp
from jax import lax
from jax.experimental import pallas as pl
from jax.experimental.pallas import tpu as pltpu
from jax.sharding import PartitionSpec as P

MESH = pl.DeviceIdType.MESH
F32 = jnp.float32
BF16 = jnp.bfloat16


def hops(step):
    return sum(min(v, 4 - v) for v in step[:3])


def send_order():
    steps = [s for s in itertools.product(range(4), range(4), range(4), range(2)) if any(s)]
    random.Random(0).shuffle(steps)
    return sorted(steps, key=lambda s: -hops(s))


ORDER = send_order()


def dot(a, b):
    return jnp.dot(a, b, preferred_element_type=F32)


def split(a):
    high = a.astype(BF16)
    return high, (a - high.astype(F32)).astype(BF16)


def iota(shape, dim):
    return lax.broadcasted_iota(jnp.int32, shape, dim)


def kernel(
    tile_s,
    block_s,
    owner_ref,
    row_ref,
    block_ref,
    atm_ref,
    wet_ref,
    kappa_ref,
    w_hbm,
    ocean_hbm,
    vert_hbm,
    ocean_out,
    atm_out,
    weights,
    planes,
    vert,
    gain,
    first,
    flux,
    masks,
    contrib,
    perm_t,
    row_out,
    row_in,
    send_f,
    recv_f,
    send_1,
    recv_1,
    send_2,
    recv_2,
    forcing,
    faces,
    edge_x,
    halo_x,
    edge_y,
    halo_y,
    coef_x,
    coef_hx,
    coef_y,
    coef_hy,
    picks,
    back,
    load_sem,
    out_sem,
    send_sem,
    recv_sem,
    halo_ss,
    halo_rs,
    ready,
):
    gx, gy = lax.axis_index("gx"), lax.axis_index("gy")
    me = gx * 8 + gy
    at_y = [((gx // 4 + d) % 4) * 4 for d in range(4)]
    at_x = [(gx % 4 + d) % 4 for d in range(4)]
    at_z = [((gy // 2 + d) % 4) * 2 for d in range(4)]
    at_c = [(gy % 2 + d) % 2 for d in range(2)]

    loads = [
        pltpu.make_async_copy(w_hbm, weights, load_sem.at[0]),
        pltpu.make_async_copy(vert_hbm, vert, load_sem.at[1]),
        pltpu.make_async_copy(ocean_hbm, planes, load_sem.at[2]),
    ]
    for copy in loads:
        copy.start()

    barrier = pltpu.get_barrier_semaphore()
    for r in range(1, 16):
        pl.semaphore_signal(barrier, inc=1, device_id=((gx + r) % 16, gy), device_id_type=MESH)
    for r in range(1, 8):
        pl.semaphore_signal(barrier, inc=1, device_id=(gx, (gy + r) % 8), device_id_type=MESH)

    def send_all(number, source, target, pitch, rows, steps, own):
        def block(ref, d):
            if pitch == 0:
                return ref.at[d]
            return ref.at[pl.ds(pl.multiple_of(d * pitch, 8), rows), :]

        if own:
            pltpu.make_async_copy(block(source, me), block(target, me), recv_sem.at[number]).start()
        for dy, dx, dz, dc in steps:
            tx, ty = at_y[dy] + at_x[dx], at_z[dz] + at_c[dc]
            pltpu.make_async_remote_copy(
                src_ref=block(source, tx * 8 + ty),
                dst_ref=block(target, me),
                send_sem=send_sem.at[number],
                recv_sem=recv_sem.at[number],
                device_id=(tx, ty),
                device_id_type=MESH,
            ).start()

    def wait_bytes(ref, sem):
        pltpu.make_async_copy(ref, ref, sem).wait()

    a = [atm_ref[i : i + 1, :] for i in range(6)]
    speed = jnp.sqrt(a[0] * a[0] + a[1] * a[1] + 0.25)
    rows4 = [
        0.5 * speed * (a[2] - a[5]),
        a[4] - 0.3 * speed * a[3],
        0.2 * speed * a[0],
        0.2 * speed * a[1],
    ]
    for b in range(48):
        flux[b] = jnp.concatenate(
            [jnp.broadcast_to(v[:, b * 128 : b * 128 + 128], (8, 128)) for v in rows4], axis=0
        ).astype(BF16)
    for i in range(8):
        masks[i] = jnp.where(iota((32, 128), 0) % 8 == i, 1.0, 0.0).astype(BF16)

    hit = (iota((128, 256), 0) == owner_ref[...]).astype(F32)
    before = (iota((256, 256), 0) < iota((256, 256), 1)).astype(BF16)
    rank = dot(hit.astype(BF16), before)
    perm = [jnp.where(rank == float(r), hit, 0.0) for r in range(4)]
    rows_f = row_ref[...].astype(F32) + 1.0
    lane128 = iota((128, 128), 1)
    row_msg = jnp.zeros((128, 128), F32)
    for r in range(4):
        at = jnp.sum(perm[r] * rows_f, axis=1, keepdims=True) - 1.0
        row_msg = jnp.where(lane128 == r, at, row_msg)
        perm_t[:, r * 128 : r * 128 + 128] = jnp.transpose(perm[r]).astype(BF16)
    row_out[...] = row_msg.reshape(128, 1, 128)

    wet = wet_ref[...].astype(F32)
    kappa = kappa_ref[...]
    row8 = iota((8, 128), 0)
    for side, r in ((0, 0), (1, 63)):
        coef_x[side] = jnp.where(row8 == 0, kappa[r : r + 1, :], wet[r : r + 1, :])
    lane = iota((64, 128), 1)
    low, high = lane == 0, lane == 127
    packed = jnp.where(low, pltpu.roll(kappa, 1, 1), pltpu.roll(wet, 2, 1))
    packed = jnp.where(lane == 2, pltpu.roll(kappa, 2, 1), packed)
    coef_y[...] = jnp.where(lane == 3, pltpu.roll(wet, 3, 1), packed)

    loads[0].wait()

    def forward(g, _):
        total = jnp.zeros((32, 128), F32)
        for i in range(8):
            p = g * 8 + i
            total = total + dot(flux[block_s[p]] * masks[i], weights[tile_s[p]])
        for c in range(4):
            contrib[pl.ds(pl.multiple_of(g * 8, 8), 8), c * 128 : c * 128 + 128] = total[
                c * 8 : c * 8 + 8
            ]
        return 0

    lax.fori_loop(0, 32, forward, 0)

    part_h, part_l = split(contrib[...])
    for r in range(4):
        pick = perm[r].astype(BF16)
        out = dot(pick, part_h) + dot(pick, part_l)
        for c in range(4):
            send_f[pl.ds(c * 4 + r, 128, stride=16), :] = out[:, c * 128 : c * 128 + 128]

    pl.semaphore_wait(barrier, 22)
    for r in range(1, 8):
        pl.semaphore_signal(ready, inc=1, device_id=(gx, (gy + r) % 8), device_id_type=MESH)

    near = [((gx + 15) % 16, gy), ((gx + 1) % 16, gy), (gx, (gy + 7) % 8), (gx, (gy + 1) % 8)]

    def swap(number, sources, targets):
        copies = []
        for side in range(4):
            copies.append(
                pltpu.make_async_remote_copy(
                    src_ref=sources[side],
                    dst_ref=targets[side ^ 1],
                    send_sem=halo_ss.at[number, side],
                    recv_sem=halo_rs.at[number, side ^ 1],
                    device_id=near[side],
                    device_id_type=MESH,
                )
            )
        for copy in copies:
            copy.start()
        return copies

    pl.semaphore_wait(ready, 7)
    send_all(0, send_f, recv_f, 16, 16, ORDER, True)
    coef_copies = swap(
        0,
        [coef_x.at[0], coef_x.at[1], coef_y, coef_y],
        [coef_hx.at[0], coef_hx.at[1], coef_hy.at[0], coef_hy.at[1]],
    )
    send_all(1, row_out, row_in, 0, 1, ORDER, True)

    loads[1].wait()
    loads[2].wait()

    def solve(i, _):
        def at(level):
            return pl.ds(pl.multiple_of(level * 64 + i * 8, 8), 8)

        kap = [vert[at(l), :] for l in range(16)]
        face = [0.5 * (kap[l] + kap[l + 1]) for l in range(15)]
        inv, upper = [], []
        for l in range(16):
            above = face[l - 1] if l > 0 else 0.0
            below = face[l] if l < 15 else 0.0
            diagonal = 1.0 + above + below
            inv.append(1.0 / (diagonal + above * upper[-1] if l > 0 else diagonal))
            upper.append(-below * inv[-1])
        for field in range(5):
            held = []
            for l in range(16):
                if field < 4:
                    value = planes[at(field * 16 + l), :]
                    value = value + face[l - 1] * held[-1] if l > 0 else value
                    held.append(value * inv[l])
                else:
                    held.append(face[l - 1] * held[-1] * inv[l] if l > 0 else inv[l])
            value = held[15]
            for l in range(15, -1, -1):
                value = held[l] - upper[l] * value if l < 15 else value
                if field < 4:
                    planes[at(field * 16 + l), :] = value
                else:
                    gain[at(l), :] = value
        return 0

    lax.fori_loop(0, 8, solve, 0)

    for copy in coef_copies:
        copy.wait()

    def edge_row(side, row, there):
        return jnp.where(there, coef_hx[side, row : row + 1, :], 0.0)

    row64 = iota((64, 128), 0)
    sides = []
    for side, shift, there, edge in (
        (0, 1, gx > 0, row64 == 0),
        (1, 63, gx < 15, row64 == 63),
    ):
        sides.append(
            [
                jnp.where(edge, edge_row(side, v, there), pltpu.roll(field, shift, 0))
                for v, field in enumerate((kappa, wet))
            ]
        )
    for side, shift, there, edge, lanes in (
        (0, 1, gy > 0, low, (0, 1)),
        (1, 127, gy < 7, high, (2, 3)),
    ):
        got = jnp.where(there, coef_hy[side], 0.0)
        goal = 0 if side == 0 else 127
        sides.append(
            [
                jnp.where(edge, pltpu.roll(got, (goal - lanes[v]) % 128, 1), pltpu.roll(field, shift, 1))
                for v, field in enumerate((kappa, wet))
            ]
        )
    for n, (kappa_n, wet_n) in enumerate(sides):
        faces[n] = 0.25 * (kappa + kappa_n) * wet * wet_n

    wait_bytes(row_in, recv_sem.at[1])
    rows_in = row_in[...].reshape(128, 128)
    rows_t = jnp.transpose(rows_in)
    x64 = iota((64, 128), 0).astype(F32)
    place = jnp.concatenate([(x64 == rows_t[r : r + 1, :]).astype(F32) for r in range(4)], axis=1)
    place = place.astype(BF16)
    twice = (lane128 % 64).astype(F32)
    fetch = [(rows_in[:, r : r + 1] == twice).astype(F32).astype(BF16) for r in range(4)]

    wait_bytes(recv_f, recv_sem.at[0])
    for c in range(4):
        got = jnp.concatenate(
            [recv_f[pl.ds(c * 4 + r, 128, stride=16), :] for r in range(4)], axis=0
        )
        got_h, got_l = split(got)
        forcing[c] = (dot(place, got_h) + dot(place, got_l)) * wet

    def mix_tracers(l, _):
        response = gain[pl.ds(pl.multiple_of(l * 64, 64), 64), :]
        for c in range(2):
            at = pl.ds(pl.multiple_of(c * 1024 + l * 64, 64), 64)
            planes[at, :] = planes[at, :] + response * forcing[c]
        return 0

    lax.fori_loop(0, 16, mix_tracers, 0)

    def send_edges(number, source):
        edge_x[number, 0] = source[pl.ds(0, 32, stride=64), :]
        edge_x[number, 1] = source[pl.ds(63, 32, stride=64), :]

        def pack(k, held):
            plane = source[pl.ds(pl.multiple_of(k * 64, 64), 64), :]
            held = jnp.where(lane == k, pltpu.roll(plane, k + 1, 1), held)
            return jnp.where(lane == k + 32, pltpu.roll(plane, k + 32, 1), held)

        edge_y[number] = lax.fori_loop(0, 32, pack, jnp.zeros((64, 128), F32))
        return swap(
            1 + number,
            [edge_x.at[number, 0], edge_x.at[number, 1], edge_y.at[number], edge_y.at[number]],
            [halo_x.at[number, 0], halo_x.at[number, 1], halo_y.at[number, 0], halo_y.at[number, 1]],
        )

    def diffuse(number, source, target, k):
        at = pl.ds(pl.multiple_of(k * 64, 64), 64)
        q = source[at, :]
        up = jnp.where(row64 == 0, halo_x[number, 0, pl.ds(k, 1), :], pltpu.roll(q, 1, 0))
        down = jnp.where(row64 == 63, halo_x[number, 1, pl.ds(k, 1), :], pltpu.roll(q, 63, 0))
        left = jnp.where(low, pltpu.roll(halo_y[number, 0], (128 - k) % 128, 1), pltpu.roll(q, 1, 1))
        right = jnp.where(high, pltpu.roll(halo_y[number, 1], 95 - k, 1), pltpu.roll(q, 127, 1))
        total = q
        for n, other in enumerate((up, down, left, right)):
            total = total + faces[n] * (other - q)
        target[at, :] = total

    def give_back(source, target, pitch):
        parts = [split(v) for v in source]
        stacked = jnp.concatenate(
            [jnp.concatenate([h, l], axis=0) for h, l in parts], axis=1
        )
        for r in range(4):
            out = dot(fetch[r], stacked)
            for c in range(len(source)):
                target[pl.ds(c * 4 + r, 128, stride=pitch), :] = out[:, c * 128 : c * 128 + 128]

    copies_1 = send_edges(0, planes)
    response = gain[0:64, :]
    give_back(
        [(planes[c * 1024 : c * 1024 + 64, :] + response * forcing[c]) * wet for c in (2, 3)] + [wet],
        send_1,
        16,
    )
    send_all(2, send_1, recv_1, 16, 12, ORDER[:64], True)
    for copy in copies_1:
        copy.wait()

    def pass_1(k, _):
        diffuse(0, planes, first, k)
        return 0

    lax.fori_loop(0, 32, pass_1, 0)
    copies_2 = send_edges(1, first)
    send_all(2, send_1, recv_1, 16, 12, ORDER[64:], False)
    for copy in copies_2:
        copy.wait()
    diffuse(1, first, planes, 0)
    diffuse(1, first, planes, 16)
    give_back([planes[c * 1024 : c * 1024 + 64, :] * wet for c in (0, 1)], send_2, 8)
    send_all(3, send_2, recv_2, 8, 8, ORDER, True)

    def pass_2(l, _):
        diffuse(1, first, planes, l)
        diffuse(1, first, planes, l + 16)
        return 0

    lax.fori_loop(1, 16, pass_2, 0)

    def mix_flow(l, _):
        response = gain[pl.ds(pl.multiple_of(l * 64, 64), 64), :]
        for c in (2, 3):
            at = pl.ds(pl.multiple_of(c * 1024 + l * 64, 64), 64)
            planes[at, :] = planes[at, :] + response * forcing[c]
        return 0

    lax.fori_loop(0, 16, mix_flow, 0)
    store = pltpu.make_async_copy(planes, ocean_out, out_sem)
    store.start()

    wait_bytes(recv_1.at[pl.ds(0, 1536), :], recv_sem.at[2])

    def take(source, pitch, c, plane):
        got = jnp.concatenate(
            [source[pl.ds(c * 4 + r, 128, stride=pitch), :] for r in range(4)], axis=0
        )
        for half, part in enumerate(split(got)):
            picks[half * 5 + plane] = dot(perm_t[...], part)

    for c, plane in ((0, 2), (1, 3), (2, 4)):
        take(recv_1, 16, c, plane)
    wait_bytes(recv_2, recv_sem.at[3])
    for c in range(2):
        take(recv_2, 8, c, c)

    row80 = iota((80, 128), 0) % 8

    def backward(g, _):
        at = pl.ds(pl.multiple_of(g * 8, 8), 8)
        rows = jnp.concatenate([picks[n, at, :] for n in range(10)], axis=0)
        total = jnp.zeros((80, 128), F32)
        for i in range(8):
            mine = jnp.where(row80 == i, rows, 0.0).astype(BF16)
            total = total + lax.dot_general(
                mine,
                weights[tile_s[g * 8 + i]],
                (((1,), (1,)), ((), ())),
                preferred_element_type=F32,
            )
        for c in range(5):
            back[c, at, :] = total[c * 8 : c * 8 + 8] + total[40 + c * 8 : 48 + c * 8]
        return 0

    lax.fori_loop(0, 32, backward, 0)

    of_block = iota((192, 256), 0) // 4 == block_ref[...]
    plane_of = iota((192, 256), 0) % 4
    num = jnp.zeros((192, 128), F32)
    for c in range(4):
        member = jnp.where(of_block & (plane_of == c), 1.0, 0.0).astype(BF16)
        for part in split(back[c]):
            num = num + dot(member, part)
    den = jnp.zeros((192, 128), F32)
    member = jnp.where(of_block, 1.0, 0.0).astype(BF16)
    for part in split(back[4]):
        den = den + dot(member, part)
    atm_out[...] = num / jnp.maximum(den, 0.1)

    wait_bytes(send_f.at[pl.ds(0, 127 * 16), :], send_sem.at[0])
    wait_bytes(row_out.at[pl.ds(0, 127)], send_sem.at[1])
    wait_bytes(send_1.at[pl.ds(0, 127 * 12), :], send_sem.at[2])
    wait_bytes(send_2.at[pl.ds(0, 127 * 8), :], send_sem.at[3])
    store.wait()


def local(
    atm_state,
    pair_block,
    pair_owner,
    pair_row,
    pair_tile,
    remap_weight,
    wet_mask,
    ocean_state,
    vert_kappa,
    horiz_kappa,
):
    vmem = pl.BlockSpec(memory_space=pltpu.VMEM)
    smem = pl.BlockSpec(memory_space=pltpu.SMEM)
    hbm = pl.BlockSpec(memory_space=pl.ANY)
    dma = pltpu.SemaphoreType.DMA

    def buffer(*shape, dtype=F32):
        return pltpu.VMEM(shape, dtype)

    ocean, atm = pl.pallas_call(
        kernel,
        out_shape=(
            jax.ShapeDtypeStruct((4096, 128), F32),
            jax.ShapeDtypeStruct((192, 128), F32),
        ),
        in_specs=[smem, smem, vmem, vmem, vmem, vmem, vmem, vmem, hbm, hbm, hbm],
        out_specs=(hbm, vmem),
        scratch_shapes=[
            buffer(128, 128, 128, dtype=BF16),
            buffer(4096, 128),
            buffer(1024, 128),
            buffer(1024, 128),
            buffer(2048, 128),
            buffer(48, 32, 128, dtype=BF16),
            buffer(8, 32, 128, dtype=BF16),
            buffer(256, 512),
            buffer(256, 512, dtype=BF16),
            buffer(128, 1, 128),
            buffer(128, 1, 128),
            buffer(2048, 128),
            buffer(2048, 128),
            buffer(2048, 128),
            buffer(2048, 128),
            buffer(1024, 128),
            buffer(1024, 128),
            buffer(4, 64, 128),
            buffer(4, 64, 128),
            buffer(2, 2, 32, 128),
            buffer(2, 2, 32, 128),
            buffer(2, 64, 128),
            buffer(2, 2, 64, 128),
            buffer(2, 8, 128),
            buffer(2, 8, 128),
            buffer(64, 128),
            buffer(2, 64, 128),
            buffer(10, 256, 128),
            buffer(5, 256, 128),
            dma((3,)),
            dma,
            dma((4,)),
            dma((4,)),
            dma((3, 4)),
            dma((3, 4)),
            pltpu.SemaphoreType.REGULAR,
        ],
        compiler_params=pltpu.CompilerParams(
            collective_id=0, has_side_effects=True, vmem_limit_bytes=40 << 20
        ),
        name="couple",
    )(
        pair_tile,
        pair_block,
        pair_owner.reshape(1, 256),
        pair_row.reshape(1, 256),
        pair_block.reshape(1, 256),
        atm_state,
        wet_mask,
        horiz_kappa,
        remap_weight,
        ocean_state.reshape(4096, 128),
        vert_kappa.reshape(1024, 128),
    )
    ocean_next = ocean.reshape(4, 16, 64, 128)
    atm_surface = atm.reshape(48, 4, 128).transpose(1, 0, 2).reshape(4, 6144)
    return (ocean_next, atm_surface)


def solution(mesh):
    placed = (
        P(None, ("gx", "gy")),
        P(("gx", "gy")),
        P(("gx", "gy"), None),
        P(("gx", "gy")),
        P(("gx", "gy")),
        P(("gx", "gy"), None, None),
        P("gx", "gy"),
        P(None, None, "gx", "gy"),
        P(None, "gx", "gy"),
        P("gx", "gy"),
    )
    return jax.shard_map(
        local,
        mesh=mesh,
        in_specs=placed,
        out_specs=(P(None, None, "gx", "gy"), P(None, ("gx", "gy"))),
        check_vma=False,
    )
```

time: 221 us -> 85 us (0.38)
  Pallas kernels: 0 us -> 72 us
  starting transfers between devices: 67.5 us -> 0 us
  local copies, waits for them, and re-layouts: 67.6 us -> 11.9 us
  waiting for transfers between devices: 40 us -> 0 us
  matrix products: 22.5 us -> 0 us
  other arithmetic: 20.5 us -> 0 us
    pallas_call x0 -> x1, Pallas kernels: none -> 72 us  [local(): pl.pallas_call(kernel, out_shape=(jax.ShapeDtypeStruct((4096, 128), F32),...]
    all_to_all x3 -> x0, waiting for transfers between devices: 34.8 us -> none  [the longest x1 28.3 us: local(): lax.all_to_all(sendback, ('gx', 'gy'), split_axis=0, concat_axis=0, tiled...]
    ppermute x12 -> x0, starting transfers between devices: 34.1 us -> none  [the longest x6 20.7 us: extended(): before = lax.ppermute(last, axis, up)]
    all_to_all x3 -> x0, starting transfers between devices: 33.4 us -> none  [the longest x1 11.5 us: local(): lax.all_to_all(out_rows, ('gx', 'gy'), split_axis=0, concat_axis=0, tiled...]
    scatter x2 -> x0, local copies, waits for them, and re-layouts: 27.4 us -> none  [the longest x1 25.9 us: local(): jnp.zeros((slot_count, 4, patch_width), jnp.float32).at[send_slot]]
    dot_general x5 -> x0, matrix products: 22.5 us -> none  [the longest x1 6.75 us: local(): jnp.einsum('pab,pcb->pca', tile_weights, picks_low, preferred_element_typ...]
    gather x4 -> x0, local copies, waits for them, and re-layouts: 17 us -> none  [the longest x1 10.9 us: local(): tile_weights = remap_weight[pair_tile]]
    slice x10 -> x0, local copies, waits for them, and re-layouts: 9.58 us -> none  [the longest x4 6.52 us: extended(): leading = lax.slice_in_dim(shard, 0, width, axis=dim)]
  transfers between devices with their start and end apart: 15 -> 0, of which waited for: 6 -> 0; matrix products, arithmetic and copies ran while one was open for 29% -> 0% of each run, Pallas kernels for 0% -> 0%
where the time goes in v2:
time: 85 us; the launch traced here: 84.6 us
  Pallas kernels  72 us (85%)
  local copies, waits for them, and re-layouts  11.9 us (14%)
    pallas_call x1, Pallas kernels, local(): pl.pallas_call(kernel, out_shape=(jax.ShapeDtypeStruct((4096, 128), F32),...  72 us
    unnamed x22, local copies, waits for them, and re-layouts  11.9 us

profile of v2, /device:TPU:1, one launch (start us, length us, event | category | flops | bytes accessed | tf_op | source)
XLA Modules:
  0.0 84.6 jit_solution(14459564192550028112)
XLA Ops:
  0.6 0.0 copy-start
  0.6 2.2 %copy-done = bf16[128,128,128]{2,1,0:T(8,128)(2,1)S(1)} copy-done((bf16[128,128,128]{2,1,0:T(8,128)(2,1)S(1)}, bf16[128,128,128]{2,1,0:T(8,128)(2,1)}, u32[]{:S(2)}) %copy-start) | copy-done | bytes 4194328
  2.8 0.0 copy-start.1
  2.8 1.6 %copy-done.1 = f32[4,16,64,128]{3,2,1,0:T(8,128)S(1)} copy-done((f32[4,16,64,128]{3,2,1,0:T(8,128)S(1)}, f32[4,16,64,128]{3,2,1,0:T(8,128)}, u32[]{:S(2)}) %copy-start.1) | copy-done | bytes 2097176
  4.4 0.0 copy-start.2
  4.4 1.0 %copy-done.2 = f32[16,64,128]{2,1,0:T(8,128)S(1)} copy-done((f32[16,64,128]{2,1,0:T(8,128)S(1)}, f32[16,64,128]{2,1,0:T(8,128)}, u32[]{:S(2)}) %copy-start.2) | copy-done | bytes 524312
  5.5 0.0 copy-start.3
  5.5 0.9 %copy-done.3 = f32[6,6144]{1,0:T(8,128)S(1)} copy-done((f32[6,6144]{1,0:T(8,128)S(1)}, f32[6,6144]{1,0:T(8,128)}, u32[]{:S(2)}) %copy-start.3) | copy-done | bytes 147480
  6.4 0.0 copy-start.4
  6.4 0.8 copy-done.4
  7.1 0.0 copy-start.5
  7.1 0.8 copy-done.5
  7.9 0.0 copy-start.6
  7.9 0.7 copy-done.6
  8.6 0.0 copy-start.7
  8.6 0.7 copy-done.7
  9.3 0.0 copy-start.8
  9.3 0.7 copy-done.8
  9.9 0.0 copy-start.9
  9.9 0.7 copy-done.9
  10.6 72.0 %couple.1 = (f32[4096,128]{1,0:T(8,128)S(1)}, f32[192,128]{1,0:T(8,128)S(1)}) custom-call(s32[256]{0:T(256)S(1)} %copy-done.7, s32[256]{0:T(256)S(1)} %copy-done.6, s32[1,256]{1,0:T(1,128)S(1)} %bitcast.16, s32[1,256]{1,0:T(1,128)S(1)} %bitcast.17, s32[1,256]{1,0:T(1,128)S(1)} %bitcast.15, f32[6,6144]{1,0:T(8,128)S(1)} %copy-done.3, ...), custom_call_target="tpu_custom_call" | custom-call | tf_op jit(solution)/shard_map/couple/pallas_call | solution.py:481
  82.6 1.3 %copy.15 = f32[4,16,64,128]{3,2,1,0:T(8,128)} copy(f32[4,16,64,128]{3,2,1,0:T(8,128)S(1)} %bitcast.12) | data formatting | bytes 4194304
  83.9 0.6 copy.16
Async XLA Ops:
  0.6 2.2 %copy-start = (bf16[128,128,128]{2,1,0:T(8,128)(2,1)S(1)}, bf16[128,128,128]{2,1,0:T(8,128)(2,1)}, u32[]{:S(2)}) copy-start(bf16[128,128,128]{2,1,0:T(8,128)(2,1)} %w_hbm.1) | copy-start | bytes 12582916
  2.8 1.6 %copy-start.1 = (f32[4,16,64,128]{3,2,1,0:T(8,128)S(1)}, f32[4,16,64,128]{3,2,1,0:T(8,128)}, u32[]{:S(2)}) copy-start(f32[4,16,64,128]{3,2,1,0:T(8,128)} %param.17) | copy-start | bytes 6291460
  4.4 1.0 %copy-start.2 = (f32[16,64,128]{2,1,0:T(8,128)S(1)}, f32[16,64,128]{2,1,0:T(8,128)}, u32[]{:S(2)}) copy-start(f32[16,64,128]{2,1,0:T(8,128)} %param.18) | copy-start | bytes 1572868
  5.5 0.9 %copy-start.3 = (f32[6,6144]{1,0:T(8,128)S(1)}, f32[6,6144]{1,0:T(8,128)}, u32[]{:S(2)}) copy-start(f32[6,6144]{1,0:T(8,128)} %atm_ref.1) | copy-start | bytes 442372
  6.4 0.8 copy-start.4
  7.1 0.8 copy-start.5
  7.9 0.7 copy-start.6
  8.6 0.7 copy-start.7
  9.3 0.7 copy-start.8
  9.9 0.7 copy-start.9

commit v3 on v2

--- a/solution.py
+++ b/solution.py
@@ -1,4 +1,3 @@
-import functools
 import itertools
 import random
 
@@ -41,6 +40,18 @@
 
 
 def kernel(
+    tile_hbm,
+    block_hbm,
+    owner_hbm,
+    row_hbm,
+    atm_hbm,
+    wet_hbm,
+    kappa_hbm,
+    w_hbm,
+    ocean_hbm,
+    vert_hbm,
+    ocean_out,
+    atm_out,
     tile_s,
     block_s,
     owner_ref,
@@ -49,24 +60,24 @@
     atm_ref,
     wet_ref,
     kappa_ref,
-    w_hbm,
-    ocean_hbm,
-    vert_hbm,
-    ocean_out,
-    atm_out,
+    atm_held,
     weights,
     planes,
     vert,
     gain,
     first,
     flux,
-    masks,
     contrib,
     perm_t,
+    row_held,
     row_out,
+    row_mid,
+    row_next,
     row_in,
     send_f,
     recv_f,
+    send_w,
+    recv_w,
     send_1,
     recv_1,
     send_2,
@@ -77,6 +88,7 @@
     halo_x,
     edge_y,
     halo_y,
+    sides_y,
     coef_x,
     coef_hx,
     coef_y,
@@ -89,6 +101,8 @@
     recv_sem,
     halo_ss,
     halo_rs,
+    row_ss,
+    row_rs,
     ready,
 ):
     gx, gy = lax.axis_index("gx"), lax.axis_index("gy")
@@ -99,9 +113,22 @@
     at_c = [(gy % 2 + d) % 2 for d in range(2)]
 
     loads = [
-        pltpu.make_async_copy(w_hbm, weights, load_sem.at[0]),
-        pltpu.make_async_copy(vert_hbm, vert, load_sem.at[1]),
-        pltpu.make_async_copy(ocean_hbm, planes, load_sem.at[2]),
+        pltpu.make_async_copy(source, target, load_sem.at[i])
+        for i, (source, target) in enumerate(
+            (
+                (owner_hbm, owner_ref),
+                (row_hbm, row_ref),
+                (atm_hbm, atm_ref),
+                (w_hbm, weights),
+                (tile_hbm, tile_s),
+                (block_hbm, block_s),
+                (block_hbm, block_ref),
+                (wet_hbm, wet_ref),
+                (kappa_hbm, kappa_ref),
+                (vert_hbm, vert),
+                (ocean_hbm, planes),
+            )
+        )
     ]
     for copy in loads:
         copy.start()
@@ -114,8 +141,6 @@
 
     def send_all(number, source, target, pitch, rows, steps, own):
         def block(ref, d):
-            if pitch == 0:
-                return ref.at[d]
             return ref.at[pl.ds(pl.multiple_of(d * pitch, 8), rows), :]
 
         if own:
@@ -134,6 +159,7 @@
     def wait_bytes(ref, sem):
         pltpu.make_async_copy(ref, ref, sem).wait()
 
+    loads[2].wait()
     a = [atm_ref[i : i + 1, :] for i in range(6)]
     speed = jnp.sqrt(a[0] * a[0] + a[1] * a[1] + 0.25)
     rows4 = [
@@ -142,13 +168,14 @@
         0.2 * speed * a[0],
         0.2 * speed * a[1],
     ]
+    blank = jnp.zeros((12, 128), F32)
     for b in range(48):
         flux[b] = jnp.concatenate(
-            [jnp.broadcast_to(v[:, b * 128 : b * 128 + 128], (8, 128)) for v in rows4], axis=0
+            [v[:, b * 128 : b * 128 + 128] for v in rows4] + [blank], axis=0
         ).astype(BF16)
-    for i in range(8):
-        masks[i] = jnp.where(iota((32, 128), 0) % 8 == i, 1.0, 0.0).astype(BF16)
-
+
+    loads[0].wait()
+    loads[1].wait()
     hit = (iota((128, 256), 0) == owner_ref[...]).astype(F32)
     before = (iota((256, 256), 0) < iota((256, 256), 1)).astype(BF16)
     rank = dot(hit.astype(BF16), before)
@@ -160,8 +187,12 @@
         at = jnp.sum(perm[r] * rows_f, axis=1, keepdims=True) - 1.0
         row_msg = jnp.where(lane128 == r, at, row_msg)
         perm_t[:, r * 128 : r * 128 + 128] = jnp.transpose(perm[r]).astype(BF16)
-    row_out[...] = row_msg.reshape(128, 1, 128)
-
+    row_held[...] = row_msg
+    for t in range(8):
+        row_out[t] = row_held[pl.ds(t, 16, stride=8), :]
+
+    loads[7].wait()
+    loads[8].wait()
     wet = wet_ref[...].astype(F32)
     kappa = kappa_ref[...]
     row8 = iota((8, 128), 0)
@@ -173,31 +204,60 @@
     packed = jnp.where(lane == 2, pltpu.roll(kappa, 2, 1), packed)
     coef_y[...] = jnp.where(lane == 3, pltpu.roll(wet, 3, 1), packed)
 
-    loads[0].wait()
+    for i in (3, 4, 5):
+        loads[i].wait()
 
     def forward(g, _):
-        total = jnp.zeros((32, 128), F32)
-        for i in range(8):
-            p = g * 8 + i
-            total = total + dot(flux[block_s[p]] * masks[i], weights[tile_s[p]])
-        for c in range(4):
-            contrib[pl.ds(pl.multiple_of(g * 8, 8), 8), c * 128 : c * 128 + 128] = total[
-                c * 8 : c * 8 + 8
-            ]
+        for i in range(16):
+            p = g * 16 + i
+            out = dot(flux[block_s[0, p]], weights[tile_s[0, p]])
+            contrib[pl.ds(pl.multiple_of(p * 8, 8), 8), :] = out[0:8]
         return 0
 
-    lax.fori_loop(0, 32, forward, 0)
-
-    part_h, part_l = split(contrib[...])
+    lax.fori_loop(0, 6, forward, 0)
+
+    pl.semaphore_wait(barrier, 22)
+    for r in range(1, 8):
+        pl.semaphore_signal(ready, inc=1, device_id=(gx, (gy + r) % 8), device_id_type=MESH)
+    pltpu.make_async_copy(row_out.at[gy], row_mid.at[gy], row_rs.at[0]).start()
+    for r in range(1, 8):
+        t = (gy + r) % 8
+        pltpu.make_async_remote_copy(
+            src_ref=row_out.at[t],
+            dst_ref=row_mid.at[gy],
+            send_sem=row_ss.at[0],
+            recv_sem=row_rs.at[0],
+            device_id=(gx, t),
+            device_id_type=MESH,
+        ).start()
+
+    lax.fori_loop(6, 16, forward, 0)
+
+    wait_bytes(row_mid, row_rs.at[0])
+    mid = row_mid[...].reshape(128, 128)
+    row_held[...] = mid
+    for t in range(16):
+        row_next[t] = row_held[pl.ds(t, 8, stride=16), :]
+    pltpu.make_async_copy(row_next.at[gx], row_in.at[gx], row_rs.at[1]).start()
+    for r in range(1, 16):
+        t = (gx + r) % 16
+        pltpu.make_async_remote_copy(
+            src_ref=row_next.at[t],
+            dst_ref=row_in.at[gx],
+            send_sem=row_ss.at[1],
+            recv_sem=row_rs.at[1],
+            device_id=(t, gy),
+            device_id_type=MESH,
+        ).start()
+
+    part_h, part_l = split(
+        jnp.concatenate([contrib[pl.ds(c, 256, stride=8), :] for c in range(4)], axis=1)
+    )
     for r in range(4):
         pick = perm[r].astype(BF16)
         out = dot(pick, part_h) + dot(pick, part_l)
         for c in range(4):
             send_f[pl.ds(c * 4 + r, 128, stride=16), :] = out[:, c * 128 : c * 128 + 128]
-
-    pl.semaphore_wait(barrier, 22)
-    for r in range(1, 8):
-        pl.semaphore_signal(ready, inc=1, device_id=(gx, (gy + r) % 8), device_id_type=MESH)
 
     near = [((gx + 15) % 16, gy), ((gx + 1) % 16, gy), (gx, (gy + 7) % 8), (gx, (gy + 1) % 8)]
 
@@ -225,10 +285,29 @@
         [coef_x.at[0], coef_x.at[1], coef_y, coef_y],
         [coef_hx.at[0], coef_hx.at[1], coef_hy.at[0], coef_hy.at[1]],
     )
-    send_all(1, row_out, row_in, 0, 1, ORDER, True)
-
-    loads[1].wait()
-    loads[2].wait()
+
+    wait_bytes(row_in, row_rs.at[1])
+    rows_in = row_in[...].reshape(128, 128)
+    rows_t = jnp.transpose(rows_in)
+    x64 = iota((64, 128), 0).astype(F32)
+    place = jnp.concatenate([(x64 == rows_t[r : r + 1, :]).astype(F32) for r in range(4)], axis=1)
+    place = place.astype(BF16)
+    twice = (lane128 % 64).astype(F32)
+    fetch = [(rows_in[:, r : r + 1] == twice).astype(F32).astype(BF16) for r in range(4)]
+
+    def give_back(source, target, pitch):
+        parts = [split(v) for v in source]
+        stacked = jnp.concatenate([jnp.concatenate([h, l], axis=0) for h, l in parts], axis=1)
+        for r in range(4):
+            out = dot(fetch[r], stacked)
+            for c in range(len(source)):
+                target[pl.ds(c * 4 + r, 128, stride=pitch), :] = out[:, c * 128 : c * 128 + 128]
+
+    give_back([wet], send_w, 8)
+    send_all(1, send_w, recv_w, 8, 4, ORDER, True)
+
+    loads[9].wait()
+    loads[10].wait()
 
     def solve(i, _):
         def at(level):
@@ -296,15 +375,6 @@
     for n, (kappa_n, wet_n) in enumerate(sides):
         faces[n] = 0.25 * (kappa + kappa_n) * wet * wet_n
 
-    wait_bytes(row_in, recv_sem.at[1])
-    rows_in = row_in[...].reshape(128, 128)
-    rows_t = jnp.transpose(rows_in)
-    x64 = iota((64, 128), 0).astype(F32)
-    place = jnp.concatenate([(x64 == rows_t[r : r + 1, :]).astype(F32) for r in range(4)], axis=1)
-    place = place.astype(BF16)
-    twice = (lane128 % 64).astype(F32)
-    fetch = [(rows_in[:, r : r + 1] == twice).astype(F32).astype(BF16) for r in range(4)]
-
     wait_bytes(recv_f, recv_sem.at[0])
     for c in range(4):
         got = jnp.concatenate(
@@ -322,64 +392,62 @@
 
     lax.fori_loop(0, 16, mix_tracers, 0)
 
+    pair = lane // 2
+
     def send_edges(number, source):
         edge_x[number, 0] = source[pl.ds(0, 32, stride=64), :]
         edge_x[number, 1] = source[pl.ds(63, 32, stride=64), :]
 
         def pack(k, held):
             plane = source[pl.ds(pl.multiple_of(k * 64, 64), 64), :]
-            held = jnp.where(lane == k, pltpu.roll(plane, k + 1, 1), held)
-            return jnp.where(lane == k + 32, pltpu.roll(plane, k + 32, 1), held)
-
-        edge_y[number] = lax.fori_loop(0, 32, pack, jnp.zeros((64, 128), F32))
+            return jnp.where(pair == k, pltpu.roll(plane, 2 * k + 1, 1), held)
+
+        edge_y[number] = lax.fori_loop(0, 32, pack, jnp.zeros((64, 128), F32), unroll=8)
         return swap(
             1 + number,
             [edge_x.at[number, 0], edge_x.at[number, 1], edge_y.at[number], edge_y.at[number]],
             [halo_x.at[number, 0], halo_x.at[number, 1], halo_y.at[number, 0], halo_y.at[number, 1]],
         )
 
+    def join_sides(number):
+        left, right = halo_y[number, 0], halo_y[number, 1]
+        sides_y[number] = jnp.where(lane % 2 == 1, pltpu.roll(left, 1, 1), pltpu.roll(right, 127, 1))
+
     def diffuse(number, source, target, k):
         at = pl.ds(pl.multiple_of(k * 64, 64), 64)
         q = source[at, :]
         up = jnp.where(row64 == 0, halo_x[number, 0, pl.ds(k, 1), :], pltpu.roll(q, 1, 0))
         down = jnp.where(row64 == 63, halo_x[number, 1, pl.ds(k, 1), :], pltpu.roll(q, 63, 0))
-        left = jnp.where(low, pltpu.roll(halo_y[number, 0], (128 - k) % 128, 1), pltpu.roll(q, 1, 1))
-        right = jnp.where(high, pltpu.roll(halo_y[number, 1], 95 - k, 1), pltpu.roll(q, 127, 1))
+        beside = pltpu.roll(sides_y[number], 127 - 2 * k, 1)
+        left = jnp.where(low, beside, pltpu.roll(q, 1, 1))
+        right = jnp.where(high, beside, pltpu.roll(q, 127, 1))
         total = q
         for n, other in enumerate((up, down, left, right)):
             total = total + faces[n] * (other - q)
         target[at, :] = total
 
-    def give_back(source, target, pitch):
-        parts = [split(v) for v in source]
-        stacked = jnp.concatenate(
-            [jnp.concatenate([h, l], axis=0) for h, l in parts], axis=1
-        )
-        for r in range(4):
-            out = dot(fetch[r], stacked)
-            for c in range(len(source)):
-                target[pl.ds(c * 4 + r, 128, stride=pitch), :] = out[:, c * 128 : c * 128 + 128]
-
     copies_1 = send_edges(0, planes)
     response = gain[0:64, :]
     give_back(
-        [(planes[c * 1024 : c * 1024 + 64, :] + response * forcing[c]) * wet for c in (2, 3)] + [wet],
+        [(planes[c * 1024 : c * 1024 + 64, :] + response * forcing[c]) * wet for c in (2, 3)],
         send_1,
-        16,
+        8,
     )
-    send_all(2, send_1, recv_1, 16, 12, ORDER[:64], True)
+    send_all(2, send_1, recv_1, 8, 8, ORDER[:64], True)
     for copy in copies_1:
         copy.wait()
+    join_sides(0)
 
     def pass_1(k, _):
         diffuse(0, planes, first, k)
         return 0
 
-    lax.fori_loop(0, 32, pass_1, 0)
+    lax.fori_loop(0, 32, pass_1, 0, unroll=4)
     copies_2 = send_edges(1, first)
-    send_all(2, send_1, recv_1, 16, 12, ORDER[64:], False)
+    send_all(2, send_1, recv_1, 8, 8, ORDER[64:], False)
     for copy in copies_2:
         copy.wait()
+    join_sides(1)
     diffuse(1, first, planes, 0)
     diffuse(1, first, planes, 16)
     give_back([planes[c * 1024 : c * 1024 + 64, :] * wet for c in (0, 1)], send_2, 8)
@@ -390,7 +458,7 @@
         diffuse(1, first, planes, l + 16)
         return 0
 
-    lax.fori_loop(1, 16, pass_2, 0)
+    lax.fori_loop(1, 16, pass_2, 0, unroll=3)
 
     def mix_flow(l, _):
         response = gain[pl.ds(pl.multiple_of(l * 64, 64), 64), :]
@@ -400,62 +468,85 @@
         return 0
 
     lax.fori_loop(0, 16, mix_flow, 0)
-    store = pltpu.make_async_copy(planes, ocean_out, out_sem)
+    store = pltpu.make_async_copy(planes, ocean_out, out_sem.at[0])
     store.start()
 
-    wait_bytes(recv_1.at[pl.ds(0, 1536), :], recv_sem.at[2])
 
     def take(source, pitch, c, plane):
         got = jnp.concatenate(
             [source[pl.ds(c * 4 + r, 128, stride=pitch), :] for r in range(4)], axis=0
         )
         for half, part in enumerate(split(got)):
-            picks[half * 5 + plane] = dot(perm_t[...], part)
-
-    for c, plane in ((0, 2), (1, 3), (2, 4)):
-        take(recv_1, 16, c, plane)
+            picks[pl.ds(half * 8 + plane, 256, stride=16), :] = dot(perm_t[...], part)
+
+    wait_bytes(recv_w.at[pl.ds(0, 512), :], recv_sem.at[1])
+    take(recv_w, 8, 0, 4)
+    wait_bytes(recv_1, recv_sem.at[2])
+    for c in range(2):
+        take(recv_1, 8, c, c + 2)
     wait_bytes(recv_2, recv_sem.at[3])
     for c in range(2):
         take(recv_2, 8, c, c)
 
-    row80 = iota((80, 128), 0) % 8
-
     def backward(g, _):
-        at = pl.ds(pl.multiple_of(g * 8, 8), 8)
-        rows = jnp.concatenate([picks[n, at, :] for n in range(10)], axis=0)
-        total = jnp.zeros((80, 128), F32)
-        for i in range(8):
-            mine = jnp.where(row80 == i, rows, 0.0).astype(BF16)
-            total = total + lax.dot_general(
-                mine,
-                weights[tile_s[g * 8 + i]],
+        for i in range(16):
+            p = g * 16 + i
+            out = lax.dot_general(
+                picks[pl.ds(pl.multiple_of(p * 16, 16), 16), :].astype(BF16),
+                weights[tile_s[0, p]],
                 (((1,), (1,)), ((), ())),
                 preferred_element_type=F32,
             )
-        for c in range(5):
-            back[c, at, :] = total[c * 8 : c * 8 + 8] + total[40 + c * 8 : 48 + c * 8]
+            back[pl.ds(pl.multiple_of(p * 8, 8), 8), :] = out[0:8] + out[8:16]
         return 0
 
-    lax.fori_loop(0, 32, backward, 0)
-
+    lax.fori_loop(0, 16, backward, 0)
+
+    loads[6].wait()
     of_block = iota((192, 256), 0) // 4 == block_ref[...]
     plane_of = iota((192, 256), 0) % 4
     num = jnp.zeros((192, 128), F32)
     for c in range(4):
         member = jnp.where(of_block & (plane_of == c), 1.0, 0.0).astype(BF16)
-        for part in split(back[c]):
+        for part in split(back[pl.ds(c, 256, stride=8), :]):
             num = num + dot(member, part)
     den = jnp.zeros((192, 128), F32)
     member = jnp.where(of_block, 1.0, 0.0).astype(BF16)
-    for part in split(back[4]):
+    for part in split(back[pl.ds(4, 256, stride=8), :]):
         den = den + dot(member, part)
-    atm_out[...] = num / jnp.maximum(den, 0.1)
+    atm_held[...] = num / jnp.maximum(den, 0.1)
+    store_atm = pltpu.make_async_copy(atm_held, atm_out, out_sem.at[1])
+    store_atm.start()
 
     wait_bytes(send_f.at[pl.ds(0, 127 * 16), :], send_sem.at[0])
-    wait_bytes(row_out.at[pl.ds(0, 127)], send_sem.at[1])
-    wait_bytes(send_1.at[pl.ds(0, 127 * 12), :], send_sem.at[2])
+    wait_bytes(row_out.at[pl.ds(0, 7)], row_ss.at[0])
+    wait_bytes(row_next.at[pl.ds(0, 15)], row_ss.at[1])
+    wait_bytes(send_w.at[pl.ds(0, 127 * 4), :], send_sem.at[1])
+    wait_bytes(send_1.at[pl.ds(0, 127 * 8), :], send_sem.at[2])
     wait_bytes(send_2.at[pl.ds(0, 127 * 8), :], send_sem.at[3])
     store.wait()
+    store_atm.wait()
+
+
+def hand_over(ocean_in, atm_in, ocean_out, atm_out, held, in_sem, out_sem):
+    parts = [pl.ds(i * 512, 512) for i in range(8)]
+    loads = [
+        pltpu.make_async_copy(ocean_in.at[at, :], held.at[at, :], in_sem.at[i])
+        for i, at in enumerate(parts)
+    ]
+    stores = [
+        pltpu.make_async_copy(held.at[at, :], ocean_out.at[at, :], out_sem.at[i])
+        for i, at in enumerate(parts)
+    ]
+    for copy in loads:
+        copy.start()
+    for b in range(48):
+        atm_out[:, b * 128 : b * 128 + 128] = atm_in[b * 4 : b * 4 + 4, :]
+    for load, store in zip(loads, stores):
+        load.wait()
+        store.start()
+    for copy in stores:
+        copy.wait()
 
 
 def local(
@@ -470,8 +561,6 @@
     vert_kappa,
     horiz_kappa,
 ):
-    vmem = pl.BlockSpec(memory_space=pltpu.VMEM)
-    smem = pl.BlockSpec(memory_space=pltpu.SMEM)
     hbm = pl.BlockSpec(memory_space=pl.ANY)
     dma = pltpu.SemaphoreType.DMA
 
@@ -484,24 +573,37 @@
             jax.ShapeDtypeStruct((4096, 128), F32),
             jax.ShapeDtypeStruct((192, 128), F32),
         ),
-        in_specs=[smem, smem, vmem, vmem, vmem, vmem, vmem, vmem, hbm, hbm, hbm],
-        out_specs=(hbm, vmem),
+        in_specs=[hbm] * 10,
+        out_specs=(hbm, hbm),
         scratch_shapes=[
+            pltpu.SMEM((1, 256), jnp.int32),
+            pltpu.SMEM((1, 256), jnp.int32),
+            buffer(1, 256, dtype=jnp.int32),
+            buffer(1, 256, dtype=jnp.int32),
+            buffer(1, 256, dtype=jnp.int32),
+            buffer(6, 6144),
+            buffer(64, 128, dtype=jnp.int32),
+            buffer(64, 128),
+            buffer(192, 128),
             buffer(128, 128, 128, dtype=BF16),
             buffer(4096, 128),
             buffer(1024, 128),
             buffer(1024, 128),
             buffer(2048, 128),
-            buffer(48, 32, 128, dtype=BF16),
-            buffer(8, 32, 128, dtype=BF16),
-            buffer(256, 512),
+            buffer(48, 16, 128, dtype=BF16),
+            buffer(2048, 128),
             buffer(256, 512, dtype=BF16),
-            buffer(128, 1, 128),
-            buffer(128, 1, 128),
+            buffer(128, 128),
+            buffer(8, 16, 128),
+            buffer(8, 16, 128),
+            buffer(16, 8, 128),
+            buffer(16, 8, 128),
             buffer(2048, 128),
             buffer(2048, 128),
-            buffer(2048, 128),
-            buffer(2048, 128),
+            buffer(1024, 128),
+            buffer(1024, 128),
+            buffer(1024, 128),
+            buffer(1024, 128),
             buffer(1024, 128),
             buffer(1024, 128),
             buffer(4, 64, 128),
@@ -510,30 +612,32 @@
             buffer(2, 2, 32, 128),
             buffer(2, 64, 128),
             buffer(2, 2, 64, 128),
+            buffer(2, 64, 128),
             buffer(2, 8, 128),
             buffer(2, 8, 128),
             buffer(64, 128),
             buffer(2, 64, 128),
-            buffer(10, 256, 128),
-            buffer(5, 256, 128),
-            dma((3,)),
-            dma,
+            buffer(4096, 128),
+            buffer(2048, 128),
+            dma((11,)),
+            dma((2,)),
             dma((4,)),
             dma((4,)),
             dma((3, 4)),
             dma((3, 4)),
+            dma((2,)),
+            dma((2,)),
             pltpu.SemaphoreType.REGULAR,
         ],
         compiler_params=pltpu.CompilerParams(
-            collective_id=0, has_side_effects=True, vmem_limit_bytes=40 << 20
+            collective_id=0, has_side_effects=True, vmem_limit_bytes=63 << 20
         ),
         name="couple",
     )(
-        pair_tile,
-        pair_block,
+        pair_tile.reshape(1, 256),
+        pair_block.reshape(1, 256),
         pair_owner.reshape(1, 256),
         pair_row.reshape(1, 256),
-        pair_block.reshape(1, 256),
         atm_state,
         wet_mask,
         horiz_kappa,
@@ -541,9 +645,19 @@
         ocean_state.reshape(4096, 128),
         vert_kappa.reshape(1024, 128),
     )
-    ocean_next = ocean.reshape(4, 16, 64, 128)
-    atm_surface = atm.reshape(48, 4, 128).transpose(1, 0, 2).reshape(4, 6144)
-    return (ocean_next, atm_surface)
+    vmem = pl.BlockSpec(memory_space=pltpu.VMEM)
+    ocean_next, atm_surface = pl.pallas_call(
+        hand_over,
+        out_shape=(
+            jax.ShapeDtypeStruct((4096, 128), F32),
+            jax.ShapeDtypeStruct((4, 6144), F32),
+        ),
+        in_specs=[hbm, vmem],
+        out_specs=(hbm, vmem),
+        scratch_shapes=[buffer(4096, 128), dma((8,)), dma((8,))],
+        name="hand_over",
+    )(ocean, atm)
+    return (ocean_next.reshape(4, 16, 64, 128), atm_surface)
 
 
 def solution(mesh):

time: 85 us -> 64.8 us (0.76)
  local copies, waits for them, and re-layouts: 11.9 us -> 0 us
  Pallas kernels: 72 us -> 64 us
    unnamed x22 -> x0, local copies, waits for them, and re-layouts: 11.9 us -> none
    pallas_call x1, Pallas kernels: 72 us -> 60.1 us  [local(): pl.pallas_call(kernel, out_shape=(jax.ShapeDtypeStruct((4096, 128), F32),...]
    pallas_call x0 -> x1, Pallas kernels: none -> 3.93 us  [local(): pl.pallas_call(hand_over, out_shape=(jax.ShapeDtypeStruct((4096, 128), F3...]
where the time goes in v3:
time: 64.8 us; the launch traced here: 64.7 us
  Pallas kernels  64 us (99%)
    pallas_call x1, Pallas kernels, local(): pl.pallas_call(kernel, out_shape=(jax.ShapeDtypeStruct((4096, 128), F32),...  60.1 us
    pallas_call x1, Pallas kernels, local(): pl.pallas_call(hand_over, out_shape=(jax.ShapeDtypeStruct((4096, 128), F3...  3.93 us

profile of v3, /device:TPU:1, one launch (start us, length us, event | category | flops | bytes accessed | tf_op | source)
XLA Modules:
  0.0 64.7 jit_solution(15269741055969374750)
XLA Ops:
  0.6 60.1 %couple.1 = (f32[4096,128]{1,0:T(8,128)}, f32[192,128]{1,0:T(8,128)}) custom-call(s32[1,256]{1,0:T(1,128)} %bitcast.9, s32[1,256]{1,0:T(1,128)} %bitcast.10, s32[1,256]{1,0:T(1,128)} %bitcast.11, s32[1,256]{1,0:T(1,128)} %bitcast.12, f32[6,6144]{1,0:T(8,128)} %atm_hbm.1, s32[64,128]{1,0:T(8,128)} %wet_hbm.1, f32[64,128]{1,0:T(8,128)} %kappa_hbm.1, ...), custom_call_target="tpu_custom_call" | custom-call | tf_op jit(solution)/shard_map/couple/pallas_call | solution.py:570
  60.7 3.9 %hand_over.1 = (f32[4096,128]{1,0:T(8,128)}, f32[4,6144]{1,0:T(4,128)}) custom-call(f32[4096,128]{1,0:T(8,128)} %get-tuple-element.6.ocean_in, f32[192,128]{1,0:T(8,128)} %get-tuple-element.7.atm_in), custom_call_target="tpu_custom_call" | custom-call | tf_op jit(solution)/shard_map/hand_over/pallas_call | solution.py:649

commit v4 on v3

--- a/solution.py
+++ b/solution.py
@@ -62,6 +62,7 @@
     kappa_ref,
     atm_held,
     weights,
+    weights_t,
     planes,
     vert,
     gain,
@@ -453,6 +454,12 @@
     give_back([planes[c * 1024 : c * 1024 + 64, :] * wet for c in (0, 1)], send_2, 8)
     send_all(3, send_2, recv_2, 8, 8, ORDER, True)
 
+    def turn(t, _):
+        weights_t[t] = jnp.transpose(weights[t])
+        return 0
+
+    lax.fori_loop(0, 128, turn, 0, unroll=8)
+
     def pass_2(l, _):
         diffuse(1, first, planes, l)
         diffuse(1, first, planes, l + 16)
@@ -491,12 +498,8 @@
     def backward(g, _):
         for i in range(16):
             p = g * 16 + i
-            out = lax.dot_general(
-                picks[pl.ds(pl.multiple_of(p * 16, 16), 16), :].astype(BF16),
-                weights[tile_s[0, p]],
-                (((1,), (1,)), ((), ())),
-                preferred_element_type=F32,
-            )
+            rows = picks[pl.ds(pl.multiple_of(p * 16, 16), 16), :].astype(BF16)
+            out = dot(rows, weights_t[tile_s[0, p]])
             back[pl.ds(pl.multiple_of(p * 8, 8), 8), :] = out[0:8] + out[8:16]
         return 0
 
@@ -528,8 +531,10 @@
     store_atm.wait()
 
 
-def hand_over(ocean_in, atm_in, ocean_out, atm_out, held, in_sem, out_sem):
-    parts = [pl.ds(i * 512, 512) for i in range(8)]
+def hand_over(ocean_in, atm_in, ocean_out, atm_out, held, atm_held, atm_done, in_sem, out_sem):
+    atm_load = pltpu.make_async_copy(atm_in, atm_held, in_sem.at[4])
+    atm_load.start()
+    parts = [pl.ds(i * 1024, 1024) for i in range(4)]
     loads = [
         pltpu.make_async_copy(ocean_in.at[at, :], held.at[at, :], in_sem.at[i])
         for i, at in enumerate(parts)
@@ -538,10 +543,13 @@
         pltpu.make_async_copy(held.at[at, :], ocean_out.at[at, :], out_sem.at[i])
         for i, at in enumerate(parts)
     ]
+    stores.append(pltpu.make_async_copy(atm_done, atm_out, out_sem.at[4]))
     for copy in loads:
         copy.start()
+    atm_load.wait()
     for b in range(48):
-        atm_out[:, b * 128 : b * 128 + 128] = atm_in[b * 4 : b * 4 + 4, :]
+        atm_done[:, b * 128 : b * 128 + 128] = atm_held[b * 4 : b * 4 + 4, :]
+    stores[4].start()
     for load, store in zip(loads, stores):
         load.wait()
         store.start()
@@ -585,6 +593,7 @@
             buffer(64, 128, dtype=jnp.int32),
             buffer(64, 128),
             buffer(192, 128),
+            buffer(128, 128, 128, dtype=BF16),
             buffer(128, 128, 128, dtype=BF16),
             buffer(4096, 128),
             buffer(1024, 128),
@@ -645,16 +654,22 @@
         ocean_state.reshape(4096, 128),
         vert_kappa.reshape(1024, 128),
     )
-    vmem = pl.BlockSpec(memory_space=pltpu.VMEM)
     ocean_next, atm_surface = pl.pallas_call(
         hand_over,
         out_shape=(
             jax.ShapeDtypeStruct((4096, 128), F32),
             jax.ShapeDtypeStruct((4, 6144), F32),
         ),
-        in_specs=[hbm, vmem],
-        out_specs=(hbm, vmem),
-        scratch_shapes=[buffer(4096, 128), dma((8,)), dma((8,))],
+        in_specs=[hbm, hbm],
+        out_specs=(hbm, hbm),
+        scratch_shapes=[
+            buffer(4096, 128),
+            buffer(192, 128),
+            buffer(4, 6144),
+            dma((5,)),
+            dma((5,)),
+        ],
+        compiler_params=pltpu.CompilerParams(vmem_limit_bytes=63 << 20),
         name="hand_over",
     )(ocean, atm)
     return (ocean_next.reshape(4, 16, 64, 128), atm_surface)

time: 64.8 us -> 61.3 us (0.946)
  Pallas kernels: 64 us -> 60.5 us
    pallas_call x1, Pallas kernels: 60.1 us -> 58 us  [local(): pl.pallas_call(kernel, out_shape=(jax.ShapeDtypeStruct((4096, 128), F32),...]
    pallas_call x1, Pallas kernels: 3.93 us -> 2.5 us  [local(): pl.pallas_call(hand_over, out_shape=(jax.ShapeDtypeStruct((4096, 128), F3...]
where the time goes in v4:
time: 61.3 us; the launch traced here: 61.2 us
  Pallas kernels  60.5 us (99%)
  between operations  0.64 us (1%)
    pallas_call x1, Pallas kernels, local(): pl.pallas_call(kernel, out_shape=(jax.ShapeDtypeStruct((4096, 128), F32),...  58 us
    pallas_call x1, Pallas kernels, local(): pl.pallas_call(hand_over, out_shape=(jax.ShapeDtypeStruct((4096, 128), F3...  2.5 us

profile of v4, /device:TPU:1, one launch (start us, length us, event | category | flops | bytes accessed | tf_op | source)
XLA Modules:
  0.0 61.2 jit_solution(15193481908144580851)
XLA Ops:
  0.6 58.0 %couple.1 = (f32[4096,128]{1,0:T(8,128)}, f32[192,128]{1,0:T(8,128)}) custom-call(s32[1,256]{1,0:T(1,128)} %bitcast.9, s32[1,256]{1,0:T(1,128)} %bitcast.10, s32[1,256]{1,0:T(1,128)} %bitcast.11, s32[1,256]{1,0:T(1,128)} %bitcast.12, f32[6,6144]{1,0:T(8,128)} %atm_hbm.1, s32[64,128]{1,0:T(8,128)} %wet_hbm.1, f32[64,128]{1,0:T(8,128)} %kappa_hbm.1, ...), custom_call_target="tpu_custom_call" | custom-call | tf_op jit(solution)/shard_map/couple/pallas_call | solution.py:578
  58.7 2.5 %hand_over.1 = (f32[4096,128]{1,0:T(8,128)}, f32[4,6144]{1,0:T(4,128)}) custom-call(f32[4096,128]{1,0:T(8,128)} %get-tuple-element.6.ocean_in, f32[192,128]{1,0:T(8,128)} %get-tuple-element.7.atm_in), custom_call_target="tpu_custom_call" | custom-call | tf_op jit(solution)/shard_map/hand_over/pallas_call | solution.py:657

commit v5 on v4

--- a/solution.py
+++ b/solution.py
@@ -108,9 +108,10 @@
 ):
     gx, gy = lax.axis_index("gx"), lax.axis_index("gy")
     me = gx * 8 + gy
-    at_y = [((gx // 4 + d) % 4) * 4 for d in range(4)]
-    at_x = [(gx % 4 + d) % 4 for d in range(4)]
-    at_z = [((gy // 2 + d) % 4) * 2 for d in range(4)]
+    way = 1 - 2 * (gy % 2)
+    at_y = [((gx // 4 + 4 + way * d) % 4) * 4 for d in range(4)]
+    at_x = [(gx % 4 + 4 + way * d) % 4 for d in range(4)]
+    at_z = [((gy // 2 + 4 + way * d) % 4) * 2 for d in range(4)]
     at_c = [(gy % 2 + d) % 2 for d in range(2)]
 
     loads = [
@@ -215,7 +216,7 @@
             contrib[pl.ds(pl.multiple_of(p * 8, 8), 8), :] = out[0:8]
         return 0
 
-    lax.fori_loop(0, 6, forward, 0)
+    lax.fori_loop(0, 1, forward, 0)
 
     pl.semaphore_wait(barrier, 22)
     for r in range(1, 8):
@@ -232,7 +233,16 @@
             device_id_type=MESH,
         ).start()
 
-    lax.fori_loop(6, 16, forward, 0)
+    lax.fori_loop(1, 16, forward, 0)
+
+    part_h, part_l = split(
+        jnp.concatenate([contrib[pl.ds(c, 256, stride=8), :] for c in range(4)], axis=1)
+    )
+    for r in range(4):
+        pick = perm[r].astype(BF16)
+        out = dot(pick, part_h) + dot(pick, part_l)
+        for c in range(4):
+            send_f[pl.ds(c * 4 + r, 128, stride=16), :] = out[:, c * 128 : c * 128 + 128]
 
     wait_bytes(row_mid, row_rs.at[0])
     mid = row_mid[...].reshape(128, 128)
@@ -250,15 +260,6 @@
             device_id=(t, gy),
             device_id_type=MESH,
         ).start()
-
-    part_h, part_l = split(
-        jnp.concatenate([contrib[pl.ds(c, 256, stride=8), :] for c in range(4)], axis=1)
-    )
-    for r in range(4):
-        pick = perm[r].astype(BF16)
-        out = dot(pick, part_h) + dot(pick, part_l)
-        for c in range(4):
-            send_f[pl.ds(c * 4 + r, 128, stride=16), :] = out[:, c * 128 : c * 128 + 128]
 
     near = [((gx + 15) % 16, gy), ((gx + 1) % 16, gy), (gx, (gy + 7) % 8), (gx, (gy + 1) % 8)]
 

time: 61.3 us -> 60 us (0.979)
  Pallas kernels: 60.5 us -> 59.2 us
    pallas_call x1, Pallas kernels: 58 us -> 56.7 us  [local(): pl.pallas_call(kernel, out_shape=(jax.ShapeDtypeStruct((4096, 128), F32),...]
where the time goes in v5:
time: 60 us; the launch traced here: 59.8 us
  Pallas kernels  59.2 us (99%)
  between operations  0.64 us (1%)
    pallas_call x1, Pallas kernels, local(): pl.pallas_call(kernel, out_shape=(jax.ShapeDtypeStruct((4096, 128), F32),...  56.7 us
    pallas_call x1, Pallas kernels, local(): pl.pallas_call(hand_over, out_shape=(jax.ShapeDtypeStruct((4096, 128), F3...  2.5 us

profile of v5, /device:TPU:1, one launch (start us, length us, event | category | flops | bytes accessed | tf_op | source)
XLA Modules:
  0.0 59.8 jit_solution(8456851837203021512)
XLA Ops:
  0.6 56.7 %couple.1 = (f32[4096,128]{1,0:T(8,128)}, f32[192,128]{1,0:T(8,128)}) custom-call(s32[1,256]{1,0:T(1,128)} %bitcast.9, s32[1,256]{1,0:T(1,128)} %bitcast.10, s32[1,256]{1,0:T(1,128)} %bitcast.11, s32[1,256]{1,0:T(1,128)} %bitcast.12, f32[6,6144]{1,0:T(8,128)} %atm_hbm.1, s32[64,128]{1,0:T(8,128)} %wet_hbm.1, f32[64,128]{1,0:T(8,128)} %kappa_hbm.1, ...), custom_call_target="tpu_custom_call" | custom-call | tf_op jit(solution)/shard_map/couple/pallas_call | solution.py:579
  57.3 2.5 %hand_over.1 = (f32[4096,128]{1,0:T(8,128)}, f32[4,6144]{1,0:T(4,128)}) custom-call(f32[4096,128]{1,0:T(8,128)} %get-tuple-element.6.ocean_in, f32[192,128]{1,0:T(8,128)} %get-tuple-element.7.atm_in), custom_call_target="tpu_custom_call" | custom-call | tf_op jit(solution)/shard_map/hand_over/pallas_call | solution.py:658

commit v6 on v5

--- a/solution.py
+++ b/solution.py
@@ -497,14 +497,14 @@
         take(recv_2, 8, c, c)
 
     def backward(g, _):
-        for i in range(16):
-            p = g * 16 + i
+        for i in range(32):
+            p = g * 32 + i
             rows = picks[pl.ds(pl.multiple_of(p * 16, 16), 16), :].astype(BF16)
             out = dot(rows, weights_t[tile_s[0, p]])
             back[pl.ds(pl.multiple_of(p * 8, 8), 8), :] = out[0:8] + out[8:16]
         return 0
 
-    lax.fori_loop(0, 16, backward, 0)
+    lax.fori_loop(0, 8, backward, 0)
 
     loads[6].wait()
     of_block = iota((192, 256), 0) // 4 == block_ref[...]

time: 60 us -> 59 us (0.983)
  Pallas kernels: 59.2 us -> 58.3 us
    pallas_call x1, Pallas kernels: 56.7 us -> 55.8 us  [local(): pl.pallas_call(kernel, out_shape=(jax.ShapeDtypeStruct((4096, 128), F32),...]
where the time goes in v6:
time: 59 us; the launch traced here: 58.9 us
  Pallas kernels  58.3 us (99%)
  between operations  0.64 us (1%)
    pallas_call x1, Pallas kernels, local(): pl.pallas_call(kernel, out_shape=(jax.ShapeDtypeStruct((4096, 128), F32),...  55.8 us
    pallas_call x1, Pallas kernels, local(): pl.pallas_call(hand_over, out_shape=(jax.ShapeDtypeStruct((4096, 128), F3...  2.5 us

profile of v6, /device:TPU:1, one launch (start us, length us, event | category | flops | bytes accessed | tf_op | source)
XLA Modules:
  0.0 58.9 jit_solution(5552545932715513995)
XLA Ops:
  0.6 55.8 %couple.1 = (f32[4096,128]{1,0:T(8,128)}, f32[192,128]{1,0:T(8,128)}) custom-call(s32[1,256]{1,0:T(1,128)} %bitcast.9, s32[1,256]{1,0:T(1,128)} %bitcast.10, s32[1,256]{1,0:T(1,128)} %bitcast.11, s32[1,256]{1,0:T(1,128)} %bitcast.12, f32[6,6144]{1,0:T(8,128)} %atm_hbm.1, s32[64,128]{1,0:T(8,128)} %wet_hbm.1, f32[64,128]{1,0:T(8,128)} %kappa_hbm.1, ...), custom_call_target="tpu_custom_call" | custom-call | tf_op jit(solution)/shard_map/couple/pallas_call | solution.py:579
  56.4 2.5 %hand_over.1 = (f32[4096,128]{1,0:T(8,128)}, f32[4,6144]{1,0:T(4,128)}) custom-call(f32[4096,128]{1,0:T(8,128)} %get-tuple-element.6.ocean_in, f32[192,128]{1,0:T(8,128)} %get-tuple-element.7.atm_in), custom_call_target="tpu_custom_call" | custom-call | tf_op jit(solution)/shard_map/hand_over/pallas_call | solution.py:658
